TPU v7x, 32 devices: a whole 2x2x4 slice. The times are simulated.
32 devices in a mesh: src: 4 (over z), row: 8 (over y, x, core).
Axes of the slice: x: 2, y: 2, z: 4, core: 2. Of those that a mesh axis runs over, the one named last changes fastest.
Arguments:
- spec_re: bfloat16 [1024, 1024], P('row'), may hold values from -18 to 18
- spec_im: bfloat16 [1024, 1024], P('row'), may hold values from -18 to 18
- target: float32 [1024, 1024], P('row'), may hold values from 0.3 to 1.5
- weights: float32 [32], P('src'), may hold values from 0.25 to 2.5
- cent_row: int32 [32], P('src'), may hold values from 128 to 895
- cent_col: int32 [32], P('src'), may hold values from 128 to 895
Outputs:
- grad_re: float32 [1024, 1024], P('row')
- grad_im: float32 [1024, 1024], P('row')
Inputs may be any that keep to these rules, and one draw needn't show every extreme that they name: Every pupil disk of radius 128 about (cent_row, cent_col) lies inside the band.
All inputs are finite; a program needn't handle non-finite values.
Results may differ from a plain program's by a relative error of at most 0.0072.
Values may be sent and summed in bfloat16 or wider, within the bound.
A program may use at most 128 MiB of HBM per device.

v0:
```python
import math

import jax
import jax.numpy as jnp
from jax import lax
from jax.sharding import PartitionSpec as P

RAD = 128
WIN = 384


def make_tables(band):
    position = jnp.arange(band, dtype=jnp.int32)
    phase = position[:, None] * position[None, :] % band
    angle = phase.astype(jnp.float32) * (2.0 * math.pi / band)
    factor = 1.0 / math.sqrt(band)
    return (
        (jnp.cos(angle) * factor).astype(jnp.bfloat16),
        (jnp.sin(angle) * factor).astype(jnp.bfloat16),
    )


def local(spec_re, spec_im, target, weights, cent_row, cent_col):
    rows_dev, band = spec_re.shape
    cols_dev = target.shape[0]
    points_dev = weights.shape[0]
    total_points = points_dev * lax.axis_size("src")
    cosine, sine = make_tables(band)
    tables_joined = jnp.concatenate([cosine, sine], axis=1)
    row_first = lax.axis_index("row") * rows_dev
    window_index = jnp.arange(WIN, dtype=jnp.int32)
    zero_value = jnp.zeros((), jnp.bfloat16)
    stacked = jnp.stack([spec_re, spec_im], axis=0)

    def window_starts(centre_cols):
        return jnp.clip(centre_cols - RAD, 0, band - WIN)

    def disk_window(first_row, row_count, centre_rows, centre_cols, starts):
        rows_here = first_row + jnp.arange(row_count, dtype=jnp.int32)
        row_gap = rows_here[None, :] - centre_rows[:, None]
        col_gap = starts[:, None] + window_index[None, :] - centre_cols[:, None]
        return row_gap[:, :, None] ** 2 + col_gap[:, None, :] ** 2 <= RAD * RAD

    col_first = lax.axis_index("row") * cols_dev
    narrow = jnp.concatenate(
        [
            lax.dynamic_slice_in_dim(cosine, col_first, cols_dev, 1),
            lax.dynamic_slice_in_dim(sine, col_first, cols_dev, 1),
        ],
        axis=1,
    )
    starts_all = window_starts(cent_col)
    narrow_windows = jax.vmap(lambda start: lax.dynamic_slice_in_dim(narrow, start, WIN, 0))(
        starts_all
    )
    spectrum_piece = lax.all_gather(stacked, "row", axis=1, tiled=True)
    inside_disk = disk_window(jnp.int32(0), spectrum_piece.shape[1], cent_row, cent_col, starts_all)
    pieces = jax.vmap(lambda start: lax.dynamic_slice_in_dim(spectrum_piece, start, WIN, 2))(
        starts_all
    )
    masked = jnp.where(inside_disk[:, None], pieces, zero_value)
    product = jnp.einsum(
        "pckl,plz->pckz", masked, narrow_windows, preferred_element_type=jnp.float32
    )
    real_part = product[:, 0, :, :cols_dev] - product[:, 1, :, cols_dev:]
    imag_part = product[:, 0, :, cols_dev:] + product[:, 1, :, :cols_dev]
    received = jnp.stack([real_part, imag_part], axis=1).astype(jnp.bfloat16)
    product = jnp.einsum(
        "pcky,kz->pcyz", received, tables_joined, preferred_element_type=jnp.float32
    )
    field_re = product[:, 0, :, :band] - product[:, 1, :, band:]
    field_im = product[:, 0, :, band:] + product[:, 1, :, :band]
    field = jnp.stack([field_re, field_im], axis=1)
    power = field[:, 0] * field[:, 0] + field[:, 1] * field[:, 1]
    local_power = jnp.sum(weights[:, None, None] * power, axis=0) / total_points
    intensity = lax.psum(local_power, "src")
    mismatch = intensity - target
    grad_field = (2.0 * weights[:, None, None, None] * mismatch[None, None] * field).astype(
        jnp.bfloat16
    )
    product = jnp.einsum(
        "pcyx,xz->pcyz", grad_field, tables_joined, preferred_element_type=jnp.float32
    )
    adj_re = product[:, 0, :, :band] + product[:, 1, :, band:]
    adj_im = product[:, 1, :, :band] - product[:, 0, :, band:]
    adjoint = jnp.stack([adj_re, adj_im], axis=1).astype(jnp.bfloat16)
    returned = lax.all_to_all(adjoint, "row", split_axis=3, concat_axis=2, tiled=True)
    starts = window_starts(cent_col)
    inside_disk = disk_window(row_first, rows_dev, cent_row, cent_col, starts)
    col_tables = jax.vmap(
        lambda start: jnp.concatenate(
            [
                lax.dynamic_slice_in_dim(cosine, start, WIN, 1),
                lax.dynamic_slice_in_dim(sine, start, WIN, 1),
            ],
            axis=1,
        )
    )(starts)
    result = jnp.einsum("pcyk,pyz->pckz", returned, col_tables, preferred_element_type=jnp.float32)
    term_re = result[:, 0, :, :WIN] + result[:, 1, :, WIN:]
    term_im = result[:, 1, :, :WIN] - result[:, 0, :, WIN:]
    zero_float = jnp.zeros((), jnp.float32)
    terms_re = jnp.where(inside_disk, term_re, zero_float)
    terms_im = jnp.where(inside_disk, term_im, zero_float)
    starts_local = window_starts(cent_col)
    local_re = jnp.zeros((rows_dev, band), jnp.float32)
    local_im = jnp.zeros((rows_dev, band), jnp.float32)
    for point in range(points_dev):
        start = starts_local[point]
        old_re = lax.dynamic_slice_in_dim(local_re, start, WIN, 1)
        old_im = lax.dynamic_slice_in_dim(local_im, start, WIN, 1)
        local_re = lax.dynamic_update_slice_in_dim(local_re, old_re + terms_re[point], start, 1)
        local_im = lax.dynamic_update_slice_in_dim(local_im, old_im + terms_im[point], start, 1)
    part_re, part_im = (
        lax.psum_scatter(local_re, "src", scatter_dimension=1, tiled=True),
        lax.psum_scatter(local_im, "src", scatter_dimension=1, tiled=True),
    )
    grad_re, grad_im = (
        lax.all_gather(part_re, "src", axis=1, tiled=True),
        lax.all_gather(part_im, "src", axis=1, tiled=True),
    )
    return (grad_re, grad_im)


def solution(mesh):
    return jax.shard_map(
        local,
        mesh=mesh,
        in_specs=(P("row", None), P("row", None), P("row", None), P("src"), P("src"), P("src")),
        out_specs=(P("row", None), P("row", None)),
        check_vma=False,
    )
```

profile of v0, /device:TPU:0, one launch (start us, length us, event | category | flops | bytes accessed | tf_op | source)
XLA Modules:
  0.0 404.5 jit_solution(814540712352654555)
XLA Ops:
  25.4 15.8 %multiply_convert_fusion = bf16[1024,1024]{1,0:T(8,128)(2,1)S(1)} fusion(), kind=kLoop, calls=%fused_computation.46 | loop fusion | flops 16777216 | bytes 2097152 | tf_op jit(solution)/shard_map/convert_element_type | solution.py:19
  41.3 15.7 %multiply_convert_fusion.1 = bf16[1024,1024]{1,0:T(8,128)(2,1)S(1)} fusion(), kind=kLoop, calls=%fused_computation.47 | loop fusion | flops 16777216 | bytes 2097152 | tf_op jit(solution)/shard_map/convert_element_type | solution.py:18
  62.3 15.6 %while.9 = (s32[]{:T(128)}, bf16[1024,256]{1,0:T(8,128)(2,1)S(1)}, s32[8,2]{0,1:T(2,128)S(1)}, bf16[8,384,256]{2,1,0:T(8,128)(2,1)}) while((s32[]{:T(128)}, bf16[1024,256]{1,0:T(8,128)(2,1)S(1)}, s32[8,2]{0,1:T(2,128)S(1)}, bf16[8,384,256]{2,1,0:T(8,128)(2,1)}) %tuple.83), condition=%wide.while_cond.1.clone, body=%wide.while_body.1.sunk.clone | while | flops 2 | bytes 394321 | solution.py:53
  77.9 37.9 %while.8 = (s32[]{:T(128)}, bf16[2,1024,1024]{2,1,0:T(8,128)(2,1)}, s32[8,3]{0,1:T(4,128)S(1)}, bf16[8,2,1024,384]{3,2,1,0:T(8,128)(2,1)}) while((s32[]{:T(128)}, bf16[2,1024,1024]{2,1,0:T(8,128)(2,1)}, s32[8,3]{0,1:T(4,128)S(1)}, bf16[8,2,1024,384]{3,2,1,0:T(8,128)(2,1)}) %tuple.80), condition=%wide.while_cond.clone, body=%wide.while_body.sunk.clone | while | flops 2 | bytes 3146841 | solution.py:58
  102.1 4.2 %bitcast_dynamic-update-slice_fusion.12 = bf16[8,2,1024,384]{3,2,1,0:T(8,128)(2,1)} fusion(bf16[8,2,1024,384]{3,2,1,0:T(8,128)(2,1)} %get-tuple-element.236, s32[]{:T(128)} %get-tuple-element.233, bf16[2,1024,1024]{2,1,0:T(8,128)(2,1)} %get-tuple-element.238, s32[]{:T(128)} %bitcast.150), kind=kLoop, calls=%fused_computation.clone.1.clone | loop fusion | bytes 3146752 | tf_op jit(solution)/shard_map/vmap()/gather
  111.6 4.2 %bitcast_dynamic-update-slice_fusion.12 = bf16[8,2,1024,384]{3,2,1,0:T(8,128)(2,1)} fusion(bf16[8,2,1024,384]{3,2,1,0:T(8,128)(2,1)} %get-tuple-element.236, s32[]{:T(128)} %get-tuple-element.233, bf16[2,1024,1024]{2,1,0:T(8,128)(2,1)} %get-tuple-element.238, s32[]{:T(128)} %bitcast.150), kind=kLoop, calls=%fused_computation.clone.1.clone | loop fusion | bytes 3146752 | tf_op jit(solution)/shard_map/vmap()/gather
  115.8 11.8 %fusion.3 = f32[8,2,1024,256]{3,2,1,0:T(8,128)} fusion(bf16[8,2,1024,384]{3,2,1,0:T(8,128)(2,1)} %get-tuple-element.9, pred[8,1024,384]{2,1,0:T(8,128)(4,1)} %add_compare_fusion, bf16[8,384,256]{2,1,0:T(8,128)(2,1)} %get-tuple-element.17), kind=kOutput, calls=%fused_computation.12 | convolution fusion | flops 3227516928 | bytes 34078720 | tf_op jit(solution)/shard_map/pckl,plz->pckz/dot_general | solution.py:62
  127.7 8.6 %fusion.16 = (bf16[8,1,1024,128]{3,2,1,0:T(8,128)(2,1)}, bf16[8,1,1024,128]{3,2,1,0:T(8,128)(2,1)}) fusion(f32[8,2,1024,256]{3,2,1,0:T(8,128)} %fusion.3), kind=kLoop, calls=%fused_computation.35 | loop fusion | flops 4194304 | bytes 20971520 | tf_op jit(solution)/shard_map/convert.2
  136.3 11.0 %fusion.17 = f32[8,2,128,2048]{3,2,1,0:T(8,128)S(1)} fusion(bf16[8,1,1024,128]{3,2,1,0:T(8,128)(2,1)} %get-tuple-element.72, bf16[8,1,1024,128]{3,2,1,0:T(8,128)(2,1)} %get-tuple-element.71, bf16[1024,1024]{1,0:T(8,128)(2,1)S(1)} %multiply_convert_fusion, bf16[1024,1024]{1,0:T(8,128)(2,1)S(1)} %copy-done.1), kind=kOutput, calls=%fused_computation.36 | convolution fusion | flops 8600420352 | bytes 25165824 | tf_op jit(solution)/shard_map/pcky,kz->pcyz/dot_general | solution.py:68
  147.3 4.6 %fusion.21 = (f32[128,1024]{1,0:T(8,128)S(1)}, f32[8,1,128,1024]{3,2,1,0:T(8,128)}, f32[8,1,128,1024]{3,2,1,0:T(8,128)}) fusion(f32[8]{0:T(128)S(1)} %copy-done.8, f32[8,2,128,2048]{3,2,1,0:T(8,128)S(1)} %fusion.17), kind=kLoop, calls=%fused_computation.43 | loop fusion | flops 7208960 | bytes 25690144 | tf_op jit(solution)/shard_map/reduce_sum | solution.py:75
  152.8 40.9 %all-reduce.5.cloned.1.call-done = f32[128,1024]{1,0:T(8,128)} async-done(((f32[128,1024]{1,0:T(8,128)}), f32[128,1024]{1,0:T(8,128)}) %all-reduce.5.cloned.1.call-update) | async-done | bytes 524304 | tf_op jit(solution)/shard_map/psum | solution.py:76
  195.6 14.5 %fusion.11 = f32[8,2,128,2048]{3,2,1,0:T(8,128)} fusion(f32[8,1,128,1024]{3,2,1,0:T(8,128)} %get-tuple-element.68, f32[8,1,128,1024]{3,2,1,0:T(8,128)} %get-tuple-element.67, f32[8,128,1024]{2,1,0:T(8,128)S(1)} %broadcast_multiply_fusion, bf16[1024,1024]{1,0:T(8,128)(2,1)S(1)} %multiply_convert_fusion, bf16[1024,1024]{1,0:T(8,128)(2,1)S(1)} %copy-done.2), kind=kOutput, calls=%fused_computation.25 | convolution fusion | flops 8604614656 | bytes 33554432 | tf_op jit(solution)/shard_map/pcyx,xz->pcyz/dot_general | solution.py:81
  210.0 6.7 %fusion.14 = (bf16[8,1,128,1024]{3,2,1,0:T(8,128)(2,1)S(1)}, bf16[8,1,128,1024]{3,2,1,0:T(8,128)(2,1)S(1)}) fusion(f32[8,2,128,2048]{3,2,1,0:T(8,128)} %fusion.11), kind=kLoop, calls=%fused_computation.29 | loop fusion | flops 4194304 | bytes 20971520 | tf_op jit(solution)/shard_map/convert
  219.0 11.2 %copy.13 = bf16[8,2,128,1024]{2,1,0,3:T(2,128)(2,1)} copy(bf16[8,2,128,1024]{3,2,1,0:T(8,128)(2,1)} %pad_maximum_fusion) | data formatting | bytes 8388608 | tf_op jit(solution)/shard_map/stack | solution.py:86
  230.2 4.6 %all-to-all-start = ((bf16[8,2,128,1024]{2,1,0,3:T(2,128)(2,1)}), bf16[8,2,128,1024]{2,1,0,3:T(2,128)(2,1)}, u32[]{:S(2)}, u32[]{:S(2)}) async-start(bf16[8,2,128,1024]{2,1,0,3:T(2,128)(2,1)} %copy.13), calls=%async_computation | async-start | bytes 8388608 | tf_op jit(solution)/shard_map/all_to_all | solution.py:87
  238.1 29.5 %while.10 = (s32[]{:T(128)}, bf16[1024,1024]{1,0:T(8,128)(2,1)}, s32[8,2]{0,1:T(2,128)S(1)}, bf16[8,1024,384]{2,1,0:T(8,128)(2,1)}) while((s32[]{:T(128)}, bf16[1024,1024]{1,0:T(8,128)(2,1)}, s32[8,2]{0,1:T(2,128)S(1)}, bf16[8,1024,384]{2,1,0:T(8,128)(2,1)}) %tuple.102), condition=%wide.while_cond.2.clone, body=%wide.while_body.2.sunk.clone | while | flops 2 | bytes 1573969 | solution.py:93
  270.7 20.0 %while.11 = (s32[]{:T(128)}, bf16[1024,1024]{1,0:T(8,128)(2,1)S(1)}, s32[8,2]{0,1:T(2,128)S(1)}, bf16[8,1024,384]{2,1,0:T(8,128)(2,1)}) while((s32[]{:T(128)}, bf16[1024,1024]{1,0:T(8,128)(2,1)S(1)}, s32[8,2]{0,1:T(2,128)S(1)}, bf16[8,1024,384]{2,1,0:T(8,128)(2,1)}) %tuple.103), condition=%wide.while_cond.3.clone, body=%wide.while_body.3.sunk.clone | while | flops 2 | bytes 1573969 | solution.py:94
  290.7 6.8 %copy.24 = bf16[8,2,128,8,128]{2,3,4,1,0:T(8,128)(2,1)} copy(bf16[8,2,128,8,128]{2,1,0,4,3:T(2,128)(2,1)} %bitcast.8) | data formatting | bytes 8388608 | tf_op jit(solution)/shard_map/all_to_all | solution.py:87
  297.5 7.3 %all_to_all.16 = bf16[8,2,1024,128]{2,3,1,0:T(8,128)(2,1)} reshape(bf16[8,2,8,128,128]{3,2,4,1,0:T(8,128)(2,1)} %bitcast.157) | data formatting | bytes 8388608 | tf_op jit(solution)/shard_map/all_to_all | solution.py:87
  304.8 7.7 %fusion = f32[8,2,128,768]{3,2,1,0:T(8,128)S(1)} fusion(bf16[8,2,1024,128]{2,3,1,0:T(8,128)(2,1)} %all_to_all.16, bf16[8,1024,384]{2,1,0:T(8,128)(2,1)} %get-tuple-element.33, bf16[8,1024,384]{2,1,0:T(8,128)(2,1)} %get-tuple-element.25), kind=kOutput, calls=%fused_computation.9 | convolution fusion | flops 3246391296 | bytes 23068672 | tf_op jit(solution)/shard_map/pcyk,pyz->pckz/dot_general | solution.py:99
  349.0 7.6 %reduce-scatter.5.cloned.1.call-done = f32[128,256]{1,0:T(8,128)} async-done(((f32[128,1024]{1,0:T(8,128)}), f32[128,256]{1,0:T(8,128)}) %reduce-scatter.5.cloned.1.call-update) | async-done | bytes 131088 | tf_op jit(solution)/shard_map/reduce_scatter | solution.py:116
  356.6 18.6 %all_gather.11 = f32[128,1024]{1,0:T(8,128)S(1)} all-gather(f32[128,256]{1,0:T(8,128)} %reduce-scatter.5.cloned.1.call-done), channel_id=1, replica_groups=mesh['src'=4,'row'=8] {'src'}, dimensions={1}, use_global_device_ids=true | all-gather | bytes 655360 | tf_op jit(solution)/shard_map/all_gather | solution.py:120
  375.2 5.0 %reduce-scatter.3.cloned.1.call-done = f32[128,256]{1,0:T(8,128)} async-done(((f32[128,1024]{1,0:T(8,128)}), f32[128,256]{1,0:T(8,128)}) %reduce-scatter.3.cloned.1.call-update) | async-done | bytes 131088 | tf_op jit(solution)/shard_map/reduce_scatter | solution.py:115
  380.2 16.2 %all_gather.10 = f32[128,1024]{1,0:T(8,128)S(1)} all-gather(f32[128,256]{1,0:T(8,128)} %reduce-scatter.3.cloned.1.call-done), channel_id=1, replica_groups=mesh['src'=4,'row'=8] {'src'}, dimensions={1}, use_global_device_ids=true | all-gather | bytes 655360 | tf_op jit(solution)/shard_map/all_gather | solution.py:119
  (182 shorter events, 152.5 us)
Async XLA Ops:
  7.2 51.4 %copy-start.9 = (s32[8]{0:T(128)S(1)}, s32[8]{0:T(128)}, u32[]{:S(2)}) copy-start(s32[8]{0:T(128)} %param.11) | copy-start | bytes 100
  7.2 51.4 %copy-start.7 = (s32[8]{0:T(128)S(1)}, s32[8]{0:T(128)}, u32[]{:S(2)}) copy-start(s32[8]{0:T(128)} %param.10) | copy-start | bytes 100
  7.2 70.7 %all-gather.2.cloned.1.call-start = ((), (), s32[]{:S(2)}) async-start(), calls=%async_computation.3 | async-start | bytes 4718592 | tf_op jit(solution)/shard_map/all_gather | solution.py:56
  9.1 184.6 %all-reduce.5.cloned.1.call-start = ((), (), s32[]{:S(2)}) async-start(), calls=%async_computation.4 | async-start | bytes 1048576 | tf_op jit(solution)/shard_map/psum | solution.py:76
  57.0 1.3 copy-start
  127.6 8.7 %copy-start.1 = (bf16[1024,1024]{1,0:T(8,128)(2,1)S(1)}, bf16[1024,1024]{1,0:T(8,128)(2,1)}, u32[]{:S(2)}) copy-start(bf16[1024,1024]{1,0:T(8,128)(2,1)} %copy-done) | copy-start | bytes 6291460
  136.3 11.0 %copy-start.8 = (f32[8]{0:T(128)S(1)}, f32[8]{0:T(128)}, u32[]{:S(2)}) copy-start(f32[8]{0:T(128)} %param.9) | copy-start | bytes 100
  147.3 46.4 %copy-start.6 = (f32[128,1024]{1,0:T(8,128)S(1)}, f32[128,1024]{1,0:T(8,128)}, u32[]{:S(2)}) copy-start(f32[128,1024]{1,0:T(8,128)} %param.8) | copy-start | bytes 1572868
  193.7 1.9 copy-start.2
  230.2 60.5 %all-to-all-start = ((bf16[8,2,128,1024]{2,1,0,3:T(2,128)(2,1)}), bf16[8,2,128,1024]{2,1,0,3:T(2,128)(2,1)}, u32[]{:S(2)}, u32[]{:S(2)}) async-start(bf16[8,2,128,1024]{2,1,0,3:T(2,128)(2,1)} %copy.13), calls=%async_computation | async-start | bytes 8388608 | tf_op jit(solution)/shard_map/all_to_all | solution.py:87
  234.8 121.8 %reduce-scatter.5.cloned.1.call-start = ((), (), s32[]{:S(2)}) async-start(), calls=%async_computation.6 | async-start | bytes 655360 | tf_op jit(solution)/shard_map/reduce_scatter | solution.py:116
  313.0 1.2 copy-start.5
  333.8 0.8 copy-start.4
  334.7 45.5 %reduce-scatter.3.cloned.1.call-start = ((), (), s32[]{:S(2)}) async-start(), calls=%async_computation.5 | async-start | bytes 655360 | tf_op jit(solution)/shard_map/reduce_scatter | solution.py:115
  348.2 0.8 copy-start.3
Sparse Core Ops, SparseCore 0:
  10.5 39.5 all-gather.1
  152.9 40.7 all-reduce.4
  334.8 21.7 reduce-scatter.4
  359.3 20.8 reduce-scatter.2
where the time goes:
time: 406 us; the launch traced here: 404 us
  local copies, waits for them, and re-layouts  166 us (41%)
  other arithmetic  71.6 us (18%)
  waiting for transfers between devices  53.5 us (13%)
  matrix products  44.9 us (11%)
  blocking collectives  34.8 us (9%)
  between operations  29.1 us (7%)
  starting transfers between devices  4.76 us (1%)
    gather x96, local copies, waits for them, and re-layouts  103 us
    psum x1, waiting for transfers between devices, local(): intensity = lax.psum(local_power, 'src')  40.9 us
    all_gather x1, blocking collectives, local(): lax.all_gather(part_im, 'src', axis=1, tiled=True)  18.6 us
    all_gather x1, blocking collectives, local(): lax.all_gather(part_re, 'src', axis=1, tiled=True)  16.2 us
    convert_element_type x1, other arithmetic, make_tables(): (jnp.sin(angle) * factor).astype(jnp.bfloat16)  15.8 us
    convert_element_type x1, other arithmetic, make_tables(): (jnp.cos(angle) * factor).astype(jnp.bfloat16)  15.7 us
    another operation x2, other arithmetic  15.3 us
    dot_general x1, matrix products, local(): jnp.einsum('pcyx,xz->pcyz', grad_field, tables_joined, preferred_element_...  14.5 us
  transfers between devices with their start and end apart: 5, of which 3 were waited for; matrix products, arithmetic and copies ran while one was open for 30% of the time, Pallas kernels for 0%

commit v1 on v0

v1 whole, which is shorter than its diff:
```python
import functools
import math

import jax
import jax.numpy as jnp
import numpy as np
from jax import lax
from jax.experimental import pallas as pl
from jax.experimental.pallas import tpu as pltpu
from jax.sharding import PartitionSpec as P

RAD = 128
LANES = 128
RADIX = 4
WIN_Q = 80
WIN_L = 384


def host_tables(band):
    position = np.arange(band, dtype=np.int64)
    phase = position[:, None] * position[None, :] % band
    angle = phase.astype(np.float32) * np.float32(2.0 * math.pi / band)
    factor = np.float32(1.0 / math.sqrt(band))
    return (
        (np.cos(angle) * factor).astype(jnp.bfloat16),
        (np.sin(angle) * factor).astype(jnp.bfloat16),
    )


def times_i(value):
    return -value[1], value[0]


def add(a, b):
    return a[0] + b[0], a[1] + b[1]


def sub(a, b):
    return a[0] - b[0], a[1] - b[1]


def main_kernel(
    total_points,
    own_rows,
    cent_row_ref,
    cent_col_ref,
    weight_ref,
    spec_ref,
    narrow_ref,
    wide_ref,
    back_ref,
    target_ref,
    out_ref,
    band_ref,
    field_ref,
    adj_ref,
    power_ref,
    grad_ref,
):
    slots = LANES // own_rows
    quarter = spec_ref.shape[2]
    groups = total_points // slots
    wide_rows = RADIX * WIN_Q

    def window(point):
        centre_row = cent_row_ref[point]
        centre_col = cent_col_ref[point]
        first_q = pl.multiple_of((centre_row - RAD) // (RADIX * 16) * 16, 16)
        first_l = pl.multiple_of((centre_col - RAD) // LANES * LANES, LANES)
        shape = (RADIX, WIN_Q, LANES)
        row_gap = (
            lax.broadcasted_iota(jnp.int32, shape, 1) * RADIX
            + lax.broadcasted_iota(jnp.int32, shape, 0)
            + (first_q * RADIX - centre_row)
        ).astype(jnp.float32)
        room = float(RAD * RAD) - row_gap * row_gap
        lane = lax.broadcasted_iota(jnp.int32, (1, 1, LANES), 2)
        masks = []
        for block in range(WIN_L // LANES):
            gap = (lane + (first_l + block * LANES - centre_col)).astype(jnp.float32)
            masks.append(gap * gap <= room)
        return first_q, first_l, masks

    def slot_lanes(slot):
        lane = lax.broadcasted_iota(jnp.int32, (1, 1, LANES), 2)
        return (lane // own_rows == slot).astype(jnp.float32).astype(jnp.bfloat16)

    band_ref[...] = jnp.zeros_like(band_ref)
    grad_ref[...] = jnp.zeros_like(grad_ref)

    def spread(point, carry):
        first_q, first_l, masks = window(point)
        inside = jnp.concatenate(
            [mask.astype(jnp.float32).astype(jnp.bfloat16) for mask in masks], axis=-1
        )
        rows = pl.ds(first_q, WIN_Q)
        cols = pl.ds(first_l, WIN_L)
        masked = jnp.concatenate(
            [
                (spec_ref[part, :, rows, cols] * inside).reshape(wide_rows, WIN_L)
                for part in range(2)
            ],
            axis=1,
        )
        table = jnp.concatenate([narrow_ref[0, :, cols], narrow_ref[1, :, cols]], axis=1)
        product = lax.dot_general(
            masked, table, (((1,), (1,)), ((), ())), preferred_element_type=jnp.float32
        ).astype(jnp.bfloat16)
        product = product.reshape(RADIX, WIN_Q, 2 * LANES)
        chosen = slot_lanes(point % slots)
        real = product[:, :, :LANES] * chosen
        imag = product[:, :, LANES:] * chosen
        base = pl.multiple_of(point // slots * (2 * LANES), 2 * LANES)
        low = pl.ds(base, LANES)
        high = pl.ds(base + LANES, LANES)
        rows_i = pl.ds(quarter + first_q, WIN_Q)
        band_ref[:, rows, low] += real
        band_ref[:, rows, high] += imag
        band_ref[:, rows_i, low] -= imag
        band_ref[:, rows_i, high] += real
        return carry

    lax.fori_loop(0, total_points, spread, 0)

    power_ref[...] = jnp.zeros_like(power_ref)

    def forward(group, carry):
        base = pl.multiple_of(group * (2 * LANES), 2 * LANES)
        cols = pl.ds(base, 2 * LANES)
        parts = []
        for residue in range(RADIX):
            product = jnp.dot(
                wide_ref[residue], band_ref[residue, :, cols], preferred_element_type=jnp.float32
            )
            parts.append((product[:, :LANES], product[:, LANES:]))
        even, odd = add(parts[0], parts[2]), add(parts[1], parts[3])
        even_gap, odd_gap = sub(parts[0], parts[2]), times_i(sub(parts[1], parts[3]))
        fields = [add(even, odd), add(even_gap, odd_gap), sub(even, odd), sub(even_gap, odd_gap)]
        weight = weight_ref[group]
        for index, (real, imag) in enumerate(fields):
            field_ref[index, :, pl.ds(base, LANES)] = real
            field_ref[index, :, pl.ds(base + LANES, LANES)] = imag
            power_ref[index] += weight * (real * real + imag * imag)
        return carry

    lax.fori_loop(0, groups, forward, 0)

    for index in range(RADIX):
        power = power_ref[index]
        shift = own_rows
        while shift < LANES:
            power = power + pltpu.roll(power, shift, 1)
            shift *= 2
        power_ref[index] = power * (2.0 / total_points) - 2.0 * target_ref[index]

    def backward(group, carry):
        base = pl.multiple_of(group * (2 * LANES), 2 * LANES)
        weight = weight_ref[group]
        grads = []
        for index in range(RADIX):
            scale = weight * power_ref[index]
            grads.append(
                (
                    scale * field_ref[index, :, pl.ds(base, LANES)],
                    scale * field_ref[index, :, pl.ds(base + LANES, LANES)],
                )
            )
        even, odd = add(grads[0], grads[2]), add(grads[1], grads[3])
        even_gap, odd_gap = sub(grads[0], grads[2]), times_i(sub(grads[1], grads[3]))
        folded = [add(even, odd), sub(even_gap, odd_gap), sub(even, odd), add(even_gap, odd_gap)]
        for residue, (real, imag) in enumerate(folded):
            real = real.astype(jnp.bfloat16)
            imag = imag.astype(jnp.bfloat16)
            operand = jnp.concatenate(
                [jnp.concatenate([real, imag], axis=1), jnp.concatenate([imag, -real], axis=1)],
                axis=0,
            )
            adj_ref[residue, :, pl.ds(base, 2 * LANES)] = jnp.dot(
                back_ref[residue], operand, preferred_element_type=jnp.float32
            ).astype(jnp.bfloat16)
        return carry

    lax.fori_loop(0, groups, backward, 0)

    def collect(point, carry):
        first_q, first_l, masks = window(point)
        rows = pl.ds(first_q, WIN_Q)
        cols = pl.ds(first_l, WIN_L)
        base = pl.multiple_of(point // slots * (2 * LANES), 2 * LANES)
        chosen = slot_lanes(point % slots)
        adjoint = adj_ref[:, rows, pl.ds(base, 2 * LANES)]
        adjoint = adjoint * jnp.concatenate([chosen, chosen], axis=-1)
        adjoint = adjoint.reshape(wide_rows, 2 * LANES)
        for part in range(2):
            term = jnp.dot(
                adjoint, narrow_ref[part, :, cols], preferred_element_type=jnp.float32
            ).reshape(RADIX, WIN_Q, WIN_L)
            for block, mask in enumerate(masks):
                where = (part, slice(None), rows, pl.ds(first_l + block * LANES, LANES))
                piece = term[:, :, block * LANES : (block + 1) * LANES]
                grad_ref[where] += jnp.where(mask, piece, 0.0)
        return carry

    lax.fori_loop(0, total_points, collect, 0)
    out_ref[...] = grad_ref[...].astype(out_ref.dtype)


def local(spec_re, spec_im, target, weights, cent_row, cent_col):
    rows_dev, band = spec_re.shape
    groups_src = lax.axis_size("src")
    points_dev = weights.shape[0]
    total_points = points_dev * groups_src
    own_rows = target.shape[0] // groups_src
    slots = LANES // own_rows
    groups = total_points // slots
    quarter = band // RADIX
    cosine, sine = host_tables(band)

    stacked = jnp.stack([spec_re, spec_im], axis=0).reshape(2, rows_dev // RADIX, RADIX, band)
    stacked = stacked.transpose(0, 2, 1, 3)
    spectrum = lax.all_gather(stacked, "row", axis=2, tiled=True)
    points = jnp.stack(
        [weights, cent_row.astype(jnp.float32), cent_col.astype(jnp.float32)], axis=0
    )
    points = lax.all_gather(points, "src", axis=1, tiled=True)
    weights_all = points[0]
    rows_all = points[1].astype(jnp.int32)
    cols_all = points[2].astype(jnp.int32)

    first_own = lax.axis_index("src") * own_rows
    first_row = lax.axis_index("row") * target.shape[0] + first_own
    cos_own = lax.dynamic_slice_in_dim(jnp.asarray(cosine), first_row, own_rows, 0)
    sin_own = lax.dynamic_slice_in_dim(jnp.asarray(sine), first_row, own_rows, 0)
    cos_many = jnp.tile(cos_own, (slots, 1))
    sin_many = jnp.tile(sin_own, (slots, 1))
    narrow = jnp.stack(
        [
            jnp.concatenate([cos_many, sin_many], axis=0),
            jnp.concatenate([-sin_many, cos_many], axis=0),
        ],
        axis=0,
    )
    cos_split = cosine[:quarter].reshape(quarter, quarter, RADIX).transpose(2, 0, 1)
    sin_split = sine[:quarter].reshape(quarter, quarter, RADIX).transpose(2, 0, 1)
    wide = jnp.asarray(np.concatenate([cos_split, sin_split], axis=2))
    back = jnp.asarray(
        np.concatenate([cos_split.transpose(0, 2, 1), sin_split.transpose(0, 2, 1)], axis=2)
    )
    target_own = lax.dynamic_slice_in_dim(target, first_own, own_rows, 0)
    target_own = jnp.tile(target_own, (slots, 1)).T.reshape(RADIX, quarter, LANES)
    weight_rows = jnp.repeat(weights_all, own_rows).reshape(groups, 1, LANES)

    vmem = pl.BlockSpec(memory_space=pltpu.VMEM)
    smem = pl.BlockSpec(memory_space=pltpu.SMEM)
    lanes_all = 2 * own_rows * total_points
    partial = pl.pallas_call(
        functools.partial(main_kernel, total_points, own_rows),
        out_shape=jax.ShapeDtypeStruct((2, RADIX, quarter, band), jnp.bfloat16),
        in_specs=[smem, smem] + [vmem] * 6,
        out_specs=vmem,
        scratch_shapes=[
            pltpu.VMEM((RADIX, 2 * quarter, lanes_all), jnp.bfloat16),
            pltpu.VMEM((RADIX, quarter, lanes_all), jnp.float32),
            pltpu.VMEM((RADIX, quarter, lanes_all), jnp.bfloat16),
            pltpu.VMEM((RADIX, quarter, LANES), jnp.float32),
            pltpu.VMEM((2, RADIX, quarter, band), jnp.float32),
        ],
        compiler_params=pltpu.CompilerParams(vmem_limit_bytes=56 * 1024 * 1024),
    )(rows_all, cols_all, weight_rows, spectrum, narrow, wide, back, target_own)

    summed = lax.psum_scatter(partial, "row", scatter_dimension=2, tiled=True)
    summed = lax.psum(summed, "src").astype(jnp.float32)
    summed = summed.transpose(0, 2, 1, 3).reshape(2, rows_dev, band)
    return summed[0], summed[1]


def solution(mesh):
    return jax.shard_map(
        local,
        mesh=mesh,
        in_specs=(P("row", None), P("row", None), P("row", None), P("src"), P("src"), P("src")),
        out_specs=(P("row", None), P("row", None)),
        check_vma=False,
    )
```

time: 406 us -> 201 us (0.50)
  local copies, waits for them, and re-layouts: 166 us -> 8.99 us
  other arithmetic: 71.6 us -> 2.74 us
  waiting for transfers between devices: 53.5 us -> 113 us
  Pallas kernels: 0 us -> 48.2 us
  matrix products: 44.9 us -> 0 us
  blocking collectives: 34.8 us -> 13.5 us
  between operations: 29.1 us -> 13.9 us
  starting transfers between devices: 4.76 us -> 0.12 us
    gather x96 -> x0, local copies, waits for them, and re-layouts: 103 us -> none
    pallas_call x0 -> x1, Pallas kernels: none -> 48.2 us  [local(): pl.pallas_call(functools.partial(main_kernel, total_points, own_rows), ou...]
    dot_general x4 -> x0, matrix products: 44.9 us -> none  [the longest x1 14.5 us: local(): jnp.einsum('pcyx,xz->pcyz', grad_field, tables_joined, preferred_element_...]
    reduce_scatter x2 -> x1, waiting for transfers between devices: 12.6 us -> 51.5 us  [local(): summed = lax.psum_scatter(partial, 'row', scatter_dimension=2, tiled=True)]
    convert_element_type x2 -> x0, other arithmetic: 31.6 us -> none  [the longest x1 15.8 us: make_tables(): (jnp.sin(angle) * factor).astype(jnp.bfloat16)]
    dynamic_update_slice x16 -> x0, local copies, waits for them, and re-layouts: 24.6 us -> none  [the longest x8 12.4 us: local(): lax.dynamic_update_slice_in_dim(local_re, old_re + terms_re[point], start...]
    all_gather x2 -> x1, blocking collectives: 34.8 us -> 13.5 us  [local(): points = lax.all_gather(points, 'src', axis=1, tiled=True)]
    all_gather x1, waiting for transfers between devices: 0.01 us -> 21.1 us  [local(): spectrum = lax.all_gather(stacked, 'row', axis=2, tiled=True)]
  transfers between devices with their start and end apart: 5 -> 3, of which waited for: 3 -> 3; matrix products, arithmetic and copies ran while one was open for 30% -> 2% of each run, Pallas kernels for 0% -> 0%
where the time goes in v1:
time: 201 us
  waiting for transfers between devices  113 us (56%)
  Pallas kernels  48.2 us (24%)
  between operations  13.9 us (7%)
  blocking collectives  13.5 us (7%)
  local copies, waits for them, and re-layouts  8.99 us (4%)
  other arithmetic  2.74 us (1%)
    reduce_scatter x1, waiting for transfers between devices, local(): summed = lax.psum_scatter(partial, 'row', scatter_dimension=2, tiled=True)  51.5 us
    pallas_call x1, Pallas kernels, local(): pl.pallas_call(functools.partial(main_kernel, total_points, own_rows), ou...  48.2 us
    psum x1, waiting for transfers between devices, local(): summed = lax.psum(summed, 'src').astype(jnp.float32)  40.8 us
    all_gather x1, waiting for transfers between devices, local(): spectrum = lax.all_gather(stacked, 'row', axis=2, tiled=True)  21.1 us
    all_gather x1, blocking collectives, local(): points = lax.all_gather(points, 'src', axis=1, tiled=True)  13.5 us
  transfers between devices with their start and end apart: 3, of which 3 were waited for; matrix products, arithmetic and copies ran while one was open for 2% of the time, Pallas kernels for 0%

profile of v1, /device:TPU:0, one launch (start us, length us, event | category | flops | bytes accessed | tf_op | source)
XLA Modules:
  0.0 200.8 jit_solution(1248974140409055493)
XLA Ops:
  7.3 1.1 stack.34
  8.4 0.1 copy.21
  8.4 1.1 stack.35
  9.5 0.1 copy.22
  9.6 0.8 maximum_bitcast_fusion
  10.6 13.5 %all-gather = f32[4,8,3]{1,2,0:T(4,128)S(1)} all-gather(f32[1,8,3]{1,2,0:T(4,128)S(1)} %maximum_bitcast_fusion.3), channel_id=1, replica_groups=mesh['src'=4,'row'=8] {'src'}, dimensions={0}, use_global_device_ids=true | all-gather | bytes 480 | tf_op jit(solution)/shard_map/all_gather | solution.py:225
  24.1 0.1 reshape.41
  24.2 0.6 slice_reduce_fusion
  24.8 0.1 broadcast_in_dim.7
  24.9 0.1 broadcast_in_dim.8
  25.0 0.7 broadcast_in_dim.9.weight_ref
  25.6 0.9 constant_dynamic-slice_fusion.1
  26.6 1.0 copy.23
  27.7 0.1 maximum_bitcast_fusion.1
  27.8 1.2 pad_maximum_fusion.narrow_ref
  29.0 21.1 %all-gather.3.cloned.1.call-done.spec_ref = bf16[2,4,256,1024]{3,2,1,0:T(8,128)(2,1)} async-done(((bf16[2,4,32,1024]{3,2,1,0:T(8,128)(2,1)}), bf16[2,4,256,1024]{3,2,1,0:T(8,128)(2,1)}) %all-gather.3.cloned.1.call-update) | async-done | bytes 4194320 | tf_op jit(solution)/shard_map/all_gather | solution.py:221
  50.0 48.2 %shard_map.113 = bf16[2,4,256,1024]{3,2,1,0:T(8,128)(2,1)} custom-call(s32[32]{0:T(128)} %get-tuple-element.8.cent_row_ref, s32[32]{0:T(128)} %get-tuple-element.7.cent_col_ref, f32[8,1,128]{2,1,0:T(1,128)} %broadcast_in_dim.9.weight_ref, bf16[2,4,256,1024]{3,2,1,0:T(8,128)(2,1)} %all-gather.3.cloned.1.call-done.spec_ref, ...), custom_call_target="tpu_custom_call" | custom-call | tf_op jit(solution)/shard_map/pallas_call | solution.py:256
  98.3 51.5 %reduce-scatter.2.cloned.1.call-done = bf16[2,4,32,1024]{3,2,1,0:T(8,128)(2,1)} async-done(((bf16[2,4,256,1024]{3,2,1,0:T(8,128)(2,1)}), bf16[2,4,32,1024]{3,2,1,0:T(8,128)(2,1)}) %reduce-scatter.2.cloned.1.call-update) | async-done | bytes 524304 | tf_op jit(solution)/shard_map/reduce_scatter | solution.py:271
  149.8 40.8 %all-reduce.2.cloned.1.call-done = bf16[2,32,4,1024]{3,1,2,0:T(8,128)(2,1)} async-done(((bf16[2,32,4,1024]{3,1,2,0:T(8,128)(2,1)}), bf16[2,32,4,1024]{3,1,2,0:T(8,128)(2,1)}) %all-reduce.2.cloned.1.call-update) | async-done | bytes 524304 | tf_op jit(solution)/shard_map/psum | solution.py:272
  190.6 1.1 fusion
  191.7 0.3 copy.25
  192.0 1.0 squeeze.10
  193.0 0.3 copy.24
  193.3 1.0 squeeze.4
  (22 shorter events, 0.3 us)
Async XLA Ops:
  7.2 19.4 %copy-start = (f32[128,1024]{1,0:T(8,128)S(1)}, f32[128,1024]{1,0:T(8,128)}, u32[]{:S(2)}) copy-start(f32[128,1024]{1,0:T(8,128)} %param.12) | copy-start | bytes 1572868
  7.2 3.3 %copy-start.2 = (s32[8]{0:T(128)S(1)}, s32[8]{0:T(128)}, u32[]{:S(2)}) copy-start(s32[8]{0:T(128)} %param.15) | copy-start | bytes 100
  7.2 3.3 %copy-start.3 = (s32[8]{0:T(128)S(1)}, s32[8]{0:T(128)}, u32[]{:S(2)}) copy-start(s32[8]{0:T(128)} %param.14) | copy-start | bytes 100
  7.2 3.4 %copy-start.1 = (f32[8]{0:T(128)S(1)}, f32[8]{0:T(128)}, u32[]{:S(2)}) copy-start(f32[8]{0:T(128)} %param.13) | copy-start | bytes 100
  7.2 42.8 %all-gather.3.cloned.1.call-start = ((), (), s32[]{:S(2)}) async-start(), calls=%async_computation.1 | async-start | bytes 4718592 | tf_op jit(solution)/shard_map/all_gather | solution.py:221
  10.5 139.3 %reduce-scatter.2.cloned.1.call-start = ((), (), s32[]{:S(2)}) async-start(), calls=%async_computation.2 | async-start | bytes 4718592 | tf_op jit(solution)/shard_map/reduce_scatter | solution.py:271
  98.3 92.3 %all-reduce.2.cloned.1.call-start = ((), (), s32[]{:S(2)}) async-start(), calls=%async_computation.3 | async-start | bytes 1048576 | tf_op jit(solution)/shard_map/psum | solution.py:272
Sparse Core Ops, SparseCore 0:
  10.6 39.4 all-gather.2
  98.4 51.3 reduce-scatter.1
  152.2 38.2 all-reduce.1

commit v2 on v1

--- a/solution.py
+++ b/solution.py
@@ -42,8 +42,7 @@
 def main_kernel(
     total_points,
     own_rows,
-    cent_row_ref,
-    cent_col_ref,
+    cent_ref,
     weight_ref,
     spec_ref,
     narrow_ref,
@@ -56,25 +55,31 @@
     adj_ref,
     power_ref,
     grad_ref,
+    product_ref,
+    scale_ref,
 ):
     slots = LANES // own_rows
-    quarter = spec_ref.shape[2]
+    quarter = spec_ref.shape[1] // RADIX
+    points_dev = total_points // cent_ref.shape[0]
     groups = total_points // slots
     wide_rows = RADIX * WIN_Q
 
-    def window(point):
-        centre_row = cent_row_ref[point]
-        centre_col = cent_col_ref[point]
+    def window(point, split):
+        centre_row = cent_ref[point // points_dev, 0, point % points_dev]
+        centre_col = cent_ref[point // points_dev, 1, point % points_dev]
         first_q = pl.multiple_of((centre_row - RAD) // (RADIX * 16) * 16, 16)
         first_l = pl.multiple_of((centre_col - RAD) // LANES * LANES, LANES)
-        shape = (RADIX, WIN_Q, LANES)
-        row_gap = (
-            lax.broadcasted_iota(jnp.int32, shape, 1) * RADIX
-            + lax.broadcasted_iota(jnp.int32, shape, 0)
-            + (first_q * RADIX - centre_row)
-        ).astype(jnp.float32)
+        if split:
+            shape = (RADIX, WIN_Q, LANES)
+            offset = lax.broadcasted_iota(jnp.int32, shape, 1) * RADIX
+            offset = offset + lax.broadcasted_iota(jnp.int32, shape, 0)
+        else:
+            shape = (wide_rows, LANES)
+            offset = lax.broadcasted_iota(jnp.int32, shape, 0)
+        row_gap = (offset + (first_q * RADIX - centre_row)).astype(jnp.float32)
         room = float(RAD * RAD) - row_gap * row_gap
-        lane = lax.broadcasted_iota(jnp.int32, (1, 1, LANES), 2)
+        flat = (1,) * (len(shape) - 1) + (LANES,)
+        lane = lax.broadcasted_iota(jnp.int32, flat, len(shape) - 1)
         masks = []
         for block in range(WIN_L // LANES):
             gap = (lane + (first_l + block * LANES - centre_col)).astype(jnp.float32)
@@ -82,42 +87,51 @@
         return first_q, first_l, masks
 
     def slot_lanes(slot):
-        lane = lax.broadcasted_iota(jnp.int32, (1, 1, LANES), 2)
-        return (lane // own_rows == slot).astype(jnp.float32).astype(jnp.bfloat16)
+        lane = lax.broadcasted_iota(jnp.int32, (1, LANES), 1)
+        return (lane // own_rows == slot).astype(jnp.float32)
+
+    scale_ref[...] = jnp.zeros_like(scale_ref)
+
+    def place_weight(point, carry):
+        weight = weight_ref[point // points_dev, 0, point % points_dev]
+        scale_ref[point // slots] += weight * slot_lanes(point % slots)
+        return carry
+
+    lax.fori_loop(0, total_points, place_weight, 0)
 
     band_ref[...] = jnp.zeros_like(band_ref)
     grad_ref[...] = jnp.zeros_like(grad_ref)
 
     def spread(point, carry):
-        first_q, first_l, masks = window(point)
+        first_q, first_l, masks = window(point, False)
         inside = jnp.concatenate(
             [mask.astype(jnp.float32).astype(jnp.bfloat16) for mask in masks], axis=-1
         )
+        rows_all = pl.ds(pl.multiple_of(first_q * RADIX, 16 * RADIX), wide_rows)
         rows = pl.ds(first_q, WIN_Q)
         cols = pl.ds(first_l, WIN_L)
         masked = jnp.concatenate(
-            [
-                (spec_ref[part, :, rows, cols] * inside).reshape(wide_rows, WIN_L)
-                for part in range(2)
-            ],
-            axis=1,
+            [spec_ref[part, rows_all, cols] * inside for part in range(2)], axis=1
         )
         table = jnp.concatenate([narrow_ref[0, :, cols], narrow_ref[1, :, cols]], axis=1)
         product = lax.dot_general(
             masked, table, (((1,), (1,)), ((), ())), preferred_element_type=jnp.float32
-        ).astype(jnp.bfloat16)
-        product = product.reshape(RADIX, WIN_Q, 2 * LANES)
+        )
+        product_ref[0] = product[:, :LANES]
+        product_ref[1] = product[:, LANES:]
         chosen = slot_lanes(point % slots)
-        real = product[:, :, :LANES] * chosen
-        imag = product[:, :, LANES:] * chosen
         base = pl.multiple_of(point // slots * (2 * LANES), 2 * LANES)
         low = pl.ds(base, LANES)
         high = pl.ds(base + LANES, LANES)
         rows_i = pl.ds(quarter + first_q, WIN_Q)
-        band_ref[:, rows, low] += real
-        band_ref[:, rows, high] += imag
-        band_ref[:, rows_i, low] -= imag
-        band_ref[:, rows_i, high] += real
+        for residue in range(RADIX):
+            picked = pl.ds(residue, WIN_Q, stride=RADIX)
+            real = (product_ref[0, picked, :] * chosen).astype(jnp.bfloat16)
+            imag = (product_ref[1, picked, :] * chosen).astype(jnp.bfloat16)
+            band_ref[residue, rows, low] += real
+            band_ref[residue, rows, high] += imag
+            band_ref[residue, rows_i, low] -= imag
+            band_ref[residue, rows_i, high] += real
         return carry
 
     lax.fori_loop(0, total_points, spread, 0)
@@ -136,7 +150,7 @@
         even, odd = add(parts[0], parts[2]), add(parts[1], parts[3])
         even_gap, odd_gap = sub(parts[0], parts[2]), times_i(sub(parts[1], parts[3]))
         fields = [add(even, odd), add(even_gap, odd_gap), sub(even, odd), sub(even_gap, odd_gap)]
-        weight = weight_ref[group]
+        weight = scale_ref[group]
         for index, (real, imag) in enumerate(fields):
             field_ref[index, :, pl.ds(base, LANES)] = real
             field_ref[index, :, pl.ds(base + LANES, LANES)] = imag
@@ -155,7 +169,7 @@
 
     def backward(group, carry):
         base = pl.multiple_of(group * (2 * LANES), 2 * LANES)
-        weight = weight_ref[group]
+        weight = scale_ref[group]
         grads = []
         for index in range(RADIX):
             scale = weight * power_ref[index]
@@ -183,13 +197,13 @@
     lax.fori_loop(0, groups, backward, 0)
 
     def collect(point, carry):
-        first_q, first_l, masks = window(point)
+        first_q, first_l, masks = window(point, True)
         rows = pl.ds(first_q, WIN_Q)
         cols = pl.ds(first_l, WIN_L)
         base = pl.multiple_of(point // slots * (2 * LANES), 2 * LANES)
-        chosen = slot_lanes(point % slots)
+        chosen = slot_lanes(point % slots).astype(jnp.bfloat16)
         adjoint = adj_ref[:, rows, pl.ds(base, 2 * LANES)]
-        adjoint = adjoint * jnp.concatenate([chosen, chosen], axis=-1)
+        adjoint = adjoint * jnp.concatenate([chosen, chosen], axis=-1)[None]
         adjoint = adjoint.reshape(wide_rows, 2 * LANES)
         for part in range(2):
             term = jnp.dot(
@@ -205,6 +219,423 @@
     out_ref[...] = grad_ref[...].astype(out_ref.dtype)
 
 
+def row_place():
+    row = lax.axis_index("row")
+    core, x, y = row % 2, row // 2 % 2, row // 4
+    mate = row + 1 - 2 * core
+    across_x = row + 2 - 4 * x
+    across_y = row + 4 - 8 * y
+    return row, core, x, y, mate, across_x, across_y
+
+
+def enter(rows, sources):
+    barrier = pltpu.get_barrier_semaphore()
+    for row in rows:
+        pl.semaphore_signal(
+            barrier, inc=1, device_id={"row": row}, device_id_type=pl.DeviceIdType.MESH
+        )
+    for source in sources:
+        pl.semaphore_signal(
+            barrier, inc=1, device_id={"src": source}, device_id_type=pl.DeviceIdType.MESH
+        )
+    pl.semaphore_wait(barrier, len(rows) + len(sources))
+
+
+def gather_kernel(
+    sources,
+    re_ref,
+    im_ref,
+    cent_ref,
+    weight_ref,
+    spec_ref,
+    cents_ref,
+    weights_ref,
+    local_sem,
+    send_sem,
+    recv_sem,
+    point_send_sem,
+    point_recv_sem,
+):
+    row, core, x, y, mate, across_x, across_y = row_place()
+    corner = across_x + across_y - row
+    mate_step = mate - row
+    rows_dev = re_ref.shape[0]
+    own = lax.axis_index("src")
+    peers = [(own + step) % sources for step in range(1, sources)]
+    enter([mate, across_x, across_y], peers)
+
+    def rows_of(device):
+        return pl.ds(pl.multiple_of(device * rows_dev, rows_dev), rows_dev)
+
+    keep = [
+        pltpu.make_async_copy(re_ref, spec_ref.at[0, rows_of(row), :], local_sem.at[0]),
+        pltpu.make_async_copy(im_ref, spec_ref.at[1, rows_of(row), :], local_sem.at[1]),
+        pltpu.make_async_copy(cent_ref, cents_ref.at[own], local_sem.at[2]),
+        pltpu.make_async_copy(weight_ref, weights_ref.at[own], local_sem.at[3]),
+    ]
+    for copy in keep:
+        copy.start()
+    small = []
+    for index, peer in enumerate(peers):
+        for kind, (source, target) in enumerate(
+            [(cent_ref, cents_ref.at[own]), (weight_ref, weights_ref.at[own])]
+        ):
+            small.append(
+                pltpu.make_async_remote_copy(
+                    src_ref=source,
+                    dst_ref=target,
+                    send_sem=point_send_sem.at[kind, index],
+                    recv_sem=point_recv_sem.at[kind, index],
+                    device_id={"src": peer},
+                    device_id_type=pl.DeviceIdType.MESH,
+                )
+            )
+    for copy in small:
+        copy.start()
+
+    sent = []
+
+    def send(part, holder, to):
+        first = holder is None
+        target = spec_ref.at[part, rows_of(row if first else holder), :]
+        index = len(sent)
+        copy = pltpu.make_async_remote_copy(
+            src_ref=(re_ref, im_ref)[part] if first else target,
+            dst_ref=target,
+            send_sem=send_sem.at[index],
+            recv_sem=recv_sem.at[index],
+            device_id={"row": to},
+            device_id_type=pl.DeviceIdType.MESH,
+        )
+        copy.start()
+        sent.append(copy)
+        return copy
+
+    re_x = send(0, None, across_x)
+    im_y = send(1, None, across_y)
+    im_x = send(1, None, across_x)
+    re_y = send(0, None, across_y)
+    send(0, None, mate)
+    send(1, None, mate)
+    re_x.wait_recv()
+    re_corner = send(0, across_x, across_y)
+    send(0, across_x, mate)
+    im_y.wait_recv()
+    im_corner = send(1, across_y, across_x)
+    send(1, across_y, mate)
+    im_x.wait_recv()
+    send(1, across_x, mate)
+    re_y.wait_recv()
+    send(0, across_y, mate)
+    re_corner.wait_recv()
+    send(0, corner, mate)
+    im_corner.wait_recv()
+    send(1, corner, mate)
+    direct = (re_x, im_y, im_x, re_y, re_corner, im_corner)
+    for copy in sent:
+        if not any(copy is other for other in direct):
+            copy.wait_recv()
+    for copy in sent:
+        copy.wait_send()
+    for copy in small:
+        copy.wait()
+    for copy in keep:
+        copy.wait()
+
+
+def reduce_kernel(
+    sources,
+    part_ref,
+    out_ref,
+    mate_in,
+    chip_sum,
+    first_re_in,
+    first_im_in,
+    first_re,
+    first_im,
+    last_re_in,
+    last_im_in,
+    left_in,
+    right_in,
+    chain,
+    final_in,
+    send_sem,
+    recv_sem,
+    up_send,
+    left_recv,
+    right_recv,
+    down_send,
+    down_recv,
+):
+    row, core, x, y, mate, across_x, across_y = row_place()
+    chunks = part_ref.shape[1]
+    own = lax.axis_index("src")
+    root = sources // 2
+    has_left = jnp.logical_and(own > 0, own <= root)
+    has_right = jnp.logical_and(own >= root, own < sources - 1)
+    peers = [(own + step) % sources for step in range(1, sources)]
+    enter([mate, across_x, across_y], peers)
+
+    @pl.when(jnp.logical_not(has_left))
+    def _():
+        left_in[...] = jnp.zeros_like(left_in)
+
+    @pl.when(jnp.logical_not(has_right))
+    def _():
+        right_in[...] = jnp.zeros_like(right_in)
+
+    def wide(value):
+        return value.astype(jnp.float32)
+
+    def row_copy(kind, chunk, source, target, to):
+        return pltpu.make_async_remote_copy(
+            src_ref=source,
+            dst_ref=target,
+            send_sem=send_sem.at[kind, chunk],
+            recv_sem=recv_sem.at[kind, chunk],
+            device_id={"row": to},
+            device_id_type=pl.DeviceIdType.MESH,
+        )
+
+    pair, step_re, step_im, end_re, end_im = {}, {}, {}, {}, {}
+    for chunk in range(chunks):
+        pair[chunk] = row_copy(
+            0, chunk, part_ref.at[:, chunk, :, :, 1 - core], mate_in.at[chunk], mate
+        )
+        pair[chunk].start()
+
+    def add_pair(chunk):
+        pair[chunk].wait_recv()
+        total = wide(part_ref[:, chunk, :, :, core]) + wide(mate_in[chunk])
+        chip_sum[chunk] = total.astype(chip_sum.dtype)
+        step_re[chunk] = row_copy(
+            1, chunk, chip_sum.at[chunk, 0, :, 1 - x], first_re_in.at[chunk], across_x
+        )
+        step_im[chunk] = row_copy(
+            2, chunk, chip_sum.at[chunk, 1, 1 - y], first_im_in.at[chunk], across_y
+        )
+        step_re[chunk].start()
+        step_im[chunk].start()
+
+    def add_first(chunk):
+        step_re[chunk].wait_recv()
+        total = wide(chip_sum[chunk, 0, :, x]) + wide(first_re_in[chunk])
+        first_re[chunk] = total.astype(first_re.dtype)
+        end_re[chunk] = row_copy(
+            3, chunk, first_re.at[chunk, 1 - y], last_re_in.at[chunk], across_y
+        )
+        end_re[chunk].start()
+        step_im[chunk].wait_recv()
+        total = wide(chip_sum[chunk, 1, y]) + wide(first_im_in[chunk])
+        first_im[chunk] = total.astype(first_im.dtype)
+        end_im[chunk] = row_copy(
+            4, chunk, first_im.at[chunk, 1 - x], last_im_in.at[chunk], across_x
+        )
+        end_im[chunk].start()
+
+    def src_copy(source, target, sent, received, to):
+        return pltpu.make_async_remote_copy(
+            src_ref=source,
+            dst_ref=target,
+            send_sem=sent,
+            recv_sem=received,
+            device_id={"src": to},
+            device_id_type=pl.DeviceIdType.MESH,
+        )
+
+    after = jnp.minimum(own + 1, sources - 1)
+    before = jnp.maximum(own - 1, 0)
+
+    def to_right(chunk):
+        return src_copy(
+            chain.at[chunk], left_in.at[chunk], up_send.at[chunk], left_recv.at[chunk], after
+        )
+
+    def to_left(chunk):
+        return src_copy(
+            chain.at[chunk], right_in.at[chunk], up_send.at[chunk], right_recv.at[chunk], before
+        )
+
+    def down_left(chunk, source):
+        return src_copy(
+            source.at[chunk],
+            final_in.at[chunk],
+            down_send.at[0, chunk],
+            down_recv.at[chunk],
+            before,
+        )
+
+    def down_right(chunk, source):
+        return src_copy(
+            source.at[chunk],
+            final_in.at[chunk],
+            down_send.at[1, chunk],
+            down_recv.at[chunk],
+            after,
+        )
+
+    def add_last(chunk):
+        end_re[chunk].wait_recv()
+        end_im[chunk].wait_recv()
+
+        @pl.when(has_left)
+        def _():
+            to_right(chunk).wait_recv()
+
+        @pl.when(has_right)
+        def _():
+            to_left(chunk).wait_recv()
+
+        real = wide(first_re[chunk, y]) + wide(last_re_in[chunk])
+        imag = wide(first_im[chunk, x]) + wide(last_im_in[chunk])
+        for part, total in enumerate((real, imag)):
+            total = total + wide(left_in[chunk, part]) + wide(right_in[chunk, part])
+            chain[chunk, part] = total.astype(chain.dtype)
+
+        @pl.when(own < root)
+        def _():
+            to_right(chunk).start()
+
+        @pl.when(own > root)
+        def _():
+            to_left(chunk).start()
+
+        @pl.when(own == root)
+        def _():
+            if root > 0:
+                down_left(chunk, chain).start()
+            if root < sources - 1:
+                down_right(chunk, chain).start()
+            out_ref[:, chunk] = chain[chunk]
+
+    def spread_final(chunk):
+        @pl.when(own < root)
+        def _():
+            down_left(chunk, final_in).wait_recv()
+
+            @pl.when(own > 0)
+            def _():
+                down_left(chunk, final_in).start()
+
+            out_ref[:, chunk] = final_in[chunk]
+
+        @pl.when(own > root)
+        def _():
+            down_right(chunk, final_in).wait_recv()
+
+            @pl.when(own < sources - 1)
+            def _():
+                down_right(chunk, final_in).start()
+
+            out_ref[:, chunk] = final_in[chunk]
+
+    stages = ((add_pair, 0), (add_first, 1), (add_last, 2), (spread_final, 4))
+    for time in range(chunks + 4):
+        for stage, lag in stages:
+            if 0 <= time - lag < chunks:
+                stage(time - lag)
+
+    for chunk in range(chunks):
+        for group in (pair, step_re, step_im, end_re, end_im):
+            group[chunk].wait_send()
+
+        @pl.when(own < root)
+        def _():
+            to_right(chunk).wait_send()
+
+            @pl.when(own > 0)
+            def _():
+                down_left(chunk, final_in).wait_send()
+
+        @pl.when(own > root)
+        def _():
+            to_left(chunk).wait_send()
+
+            @pl.when(own < sources - 1)
+            def _():
+                down_right(chunk, final_in).wait_send()
+
+        @pl.when(own == root)
+        def _():
+            if root > 0:
+                down_left(chunk, chain).wait_send()
+            if root < sources - 1:
+                down_right(chunk, chain).wait_send()
+
+
+def gather_all(spec_re, spec_im, cents, weights, sources, kernels):
+    rows_dev, band = spec_re.shape
+    if not kernels:
+        spectrum = lax.all_gather(jnp.stack([spec_re, spec_im]), "row", axis=1, tiled=True)
+        return spectrum, lax.all_gather(cents, "src"), lax.all_gather(weights, "src")
+    hbm = pl.BlockSpec(memory_space=pl.ANY)
+    vmem = pl.BlockSpec(memory_space=pltpu.VMEM)
+    dma = pltpu.SemaphoreType.DMA
+    return pl.pallas_call(
+        functools.partial(gather_kernel, sources),
+        out_shape=(
+            jax.ShapeDtypeStruct((2, rows_dev * lax.axis_size("row"), band), spec_re.dtype),
+            jax.ShapeDtypeStruct((sources,) + cents.shape, cents.dtype),
+            jax.ShapeDtypeStruct((sources,) + weights.shape, weights.dtype),
+        ),
+        in_specs=[hbm, hbm, vmem, vmem],
+        out_specs=(hbm, vmem, vmem),
+        scratch_shapes=[
+            dma((4,)),
+            dma((14,)),
+            dma((14,)),
+            dma((2, max(sources - 1, 1))),
+            dma((2, max(sources - 1, 1))),
+        ],
+        compiler_params=pltpu.CompilerParams(collective_id=0, has_side_effects=True),
+    )(spec_re, spec_im, cents, weights)
+
+
+def reduce_all(partial, sources, kernels):
+    _, residues, quarter, band = partial.shape
+    if not kernels:
+        summed = lax.psum_scatter(partial, "row", scatter_dimension=2, tiled=True)
+        return lax.psum(summed, "src")
+    own = quarter // lax.axis_size("row")
+    partial = partial.reshape(2, residues, 2, 2, 2, own, band)
+    vmem = pl.BlockSpec(memory_space=pltpu.VMEM)
+    dma = pltpu.SemaphoreType.DMA
+
+    def buffer(*lead):
+        return pltpu.VMEM((residues,) + lead + (own, band), partial.dtype)
+
+    return pl.pallas_call(
+        functools.partial(reduce_kernel, sources),
+        out_shape=jax.ShapeDtypeStruct((2, residues, own, band), partial.dtype),
+        in_specs=[vmem],
+        out_specs=vmem,
+        scratch_shapes=[
+            buffer(2, 2, 2),
+            buffer(2, 2, 2),
+            buffer(2),
+            buffer(2),
+            buffer(2),
+            buffer(2),
+            buffer(),
+            buffer(),
+            buffer(2),
+            buffer(2),
+            buffer(2),
+            buffer(2),
+            dma((5, residues)),
+            dma((5, residues)),
+            dma((residues,)),
+            dma((residues,)),
+            dma((residues,)),
+            dma((2, residues)),
+            dma((residues,)),
+        ],
+        compiler_params=pltpu.CompilerParams(
+            collective_id=1, has_side_effects=True, vmem_limit_bytes=40 * 1024 * 1024
+        ),
+    )(partial)
+
+
 def local(spec_re, spec_im, target, weights, cent_row, cent_col):
     rows_dev, band = spec_re.shape
     groups_src = lax.axis_size("src")
@@ -216,16 +647,13 @@
     quarter = band // RADIX
     cosine, sine = host_tables(band)
 
-    stacked = jnp.stack([spec_re, spec_im], axis=0).reshape(2, rows_dev // RADIX, RADIX, band)
-    stacked = stacked.transpose(0, 2, 1, 3)
-    spectrum = lax.all_gather(stacked, "row", axis=2, tiled=True)
-    points = jnp.stack(
-        [weights, cent_row.astype(jnp.float32), cent_col.astype(jnp.float32)], axis=0
+    kernels = lax.axis_size("row") == 8 and rows_dev % (RADIX * 16) == 0
+    cents = jnp.stack([cent_row, cent_col], axis=0)
+    cents = jnp.pad(cents, ((0, 6), (0, LANES - points_dev)))
+    weights_wide = jnp.pad(weights[None], ((0, 7), (0, LANES - points_dev)))
+    spectrum, cents_all, weights_all = gather_all(
+        spec_re, spec_im, cents, weights_wide, groups_src, kernels
     )
-    points = lax.all_gather(points, "src", axis=1, tiled=True)
-    weights_all = points[0]
-    rows_all = points[1].astype(jnp.int32)
-    cols_all = points[2].astype(jnp.int32)
 
     first_own = lax.axis_index("src") * own_rows
     first_row = lax.axis_index("row") * target.shape[0] + first_own
@@ -248,7 +676,6 @@
     )
     target_own = lax.dynamic_slice_in_dim(target, first_own, own_rows, 0)
     target_own = jnp.tile(target_own, (slots, 1)).T.reshape(RADIX, quarter, LANES)
-    weight_rows = jnp.repeat(weights_all, own_rows).reshape(groups, 1, LANES)
 
     vmem = pl.BlockSpec(memory_space=pltpu.VMEM)
     smem = pl.BlockSpec(memory_space=pltpu.SMEM)
@@ -256,7 +683,7 @@
     partial = pl.pallas_call(
         functools.partial(main_kernel, total_points, own_rows),
         out_shape=jax.ShapeDtypeStruct((2, RADIX, quarter, band), jnp.bfloat16),
-        in_specs=[smem, smem] + [vmem] * 6,
+        in_specs=[smem, smem] + [vmem] * 5,
         out_specs=vmem,
         scratch_shapes=[
             pltpu.VMEM((RADIX, 2 * quarter, lanes_all), jnp.bfloat16),
@@ -264,12 +691,13 @@
             pltpu.VMEM((RADIX, quarter, lanes_all), jnp.bfloat16),
             pltpu.VMEM((RADIX, quarter, LANES), jnp.float32),
             pltpu.VMEM((2, RADIX, quarter, band), jnp.float32),
+            pltpu.VMEM((2, RADIX * WIN_Q, LANES), jnp.float32),
+            pltpu.VMEM((groups, 1, LANES), jnp.float32),
         ],
         compiler_params=pltpu.CompilerParams(vmem_limit_bytes=56 * 1024 * 1024),
-    )(rows_all, cols_all, weight_rows, spectrum, narrow, wide, back, target_own)
-
-    summed = lax.psum_scatter(partial, "row", scatter_dimension=2, tiled=True)
-    summed = lax.psum(summed, "src").astype(jnp.float32)
+    )(cents_all, weights_all, spectrum, narrow, wide, back, target_own)
+
+    summed = reduce_all(partial, groups_src, kernels).astype(jnp.float32)
     summed = summed.transpose(0, 2, 1, 3).reshape(2, rows_dev, band)
     return summed[0], summed[1]
 

time: 201 us -> 135 us (0.67)
  waiting for transfers between devices: 113 us -> 0 us
  Pallas kernels: 48.2 us -> 123 us
  blocking collectives: 13.5 us -> 0 us
  between operations: 13.9 us -> 0.74 us
    pallas_call x0 -> x2, Pallas kernels: none -> 73.8 us  [the longest x1 46 us: reduce_all(): pl.pallas_call(functools.partial(reduce_kernel, sources), out_shape=jax.S...]
    reduce_scatter x1 -> x0, waiting for transfers between devices: 51.5 us -> none  [local(): summed = lax.psum_scatter(partial, 'row', scatter_dimension=2, tiled=True)]
    psum x1 -> x0, waiting for transfers between devices: 40.8 us -> none  [local(): summed = lax.psum(summed, 'src').astype(jnp.float32)]
    all_gather x1 -> x0, waiting for transfers between devices: 21.1 us -> none  [local(): spectrum = lax.all_gather(stacked, 'row', axis=2, tiled=True)]
    all_gather x1 -> x0, blocking collectives: 13.5 us -> none  [local(): points = lax.all_gather(points, 'src', axis=1, tiled=True)]
    another operation x4 -> x0, local copies, waits for them, and re-layouts: 2.32 us -> none  [local(): jnp.stack([spec_re, spec_im], axis=0)]
    unnamed x9 -> x4, local copies, waits for them, and re-layouts: 0.11 us -> 2.2 us
  transfers between devices with their start and end apart: 3 -> 0, of which waited for: 3 -> 0; matrix products, arithmetic and copies ran while one was open for 2% -> 0% of each run, Pallas kernels for 0% -> 0%
where the time goes in v2:
time: 135 us
  Pallas kernels  123 us (91%)
  local copies, waits for them, and re-layouts  8.73 us (6%)
  other arithmetic  2.12 us (2%)
    pallas_call x1, Pallas kernels, local(): pl.pallas_call(functools.partial(main_kernel, total_points, own_rows), ou...  49.5 us
    pallas_call x1, Pallas kernels, reduce_all(): pl.pallas_call(functools.partial(reduce_kernel, sources), out_shape=jax.S...  46 us
    pallas_call x1, Pallas kernels, gather_all(): pl.pallas_call(functools.partial(gather_kernel, sources), out_shape=(jax....  27.7 us

profile of v2, /device:TPU:0, one launch (start us, length us, event | category | flops | bytes accessed | tf_op | source)
XLA Modules:
  0.0 134.9 jit_solution(15834144443702103722)
XLA Ops:
  0.6 0.0 copy-start
  0.7 0.7 pad_add_fusion
  1.4 0.6 pad.8.cent_ref
  2.0 1.2 pad.9.weight_ref
  3.2 0.0 copy-done
  3.3 0.9 constant_dynamic-slice_fusion.1
  4.2 0.1 maximum_bitcast_fusion
  4.4 1.1 pad_maximum_fusion.narrow_ref
  5.5 1.0 copy.13
  6.5 27.7 %shard_map.113 = (bf16[2,1024,1024]{2,1,0:T(8,128)(2,1)}, s32[4,8,128]{2,1,0:T(8,128)}, f32[4,8,128]{2,1,0:T(8,128)}) custom-call(bf16[128,1024]{1,0:T(8,128)(2,1)} %re_ref.1, bf16[128,1024]{1,0:T(8,128)(2,1)} %im_ref.1, s32[8,128]{1,0:T(8,128)} %pad.8.cent_ref, f32[8,128]{1,0:T(8,128)} %pad.9.weight_ref), custom_call_target="tpu_custom_call" | custom-call | tf_op jit(solution)/shard_map/pallas_call | solution.py:574
  34.3 49.5 %shard_map.114 = bf16[2,4,256,1024]{3,2,1,0:T(8,128)(2,1)} custom-call(s32[4,8,128]{2,1,0:T(8,128)} %get-tuple-element.5.cent_ref, f32[4,8,128]{2,1,0:T(8,128)} %get-tuple-element.6.weight_ref, bf16[2,1024,1024]{2,1,0:T(8,128)(2,1)} %get-tuple-element.7.spec_ref, bf16[2,256,1024]{2,1,0:T(8,128)(2,1)} %pad_maximum_fusion.narrow_ref, ...), custom_call_target="tpu_custom_call" | custom-call | tf_op jit(solution)/shard_map/pallas_call | solution.py:683
  83.8 0.0 copy-start.1
  83.8 2.2 %copy-done.1 = bf16[2,4,256,1024]{3,2,1,0:T(8,128)(2,1)S(1)} copy-done((bf16[2,4,256,1024]{3,2,1,0:T(8,128)(2,1)S(1)}, bf16[2,4,256,1024]{3,2,1,0:T(8,128)(2,1)}, u32[]{:S(2)}) %copy-start.1) | copy-done | bytes 4194328
  86.0 46.0 %shard_map.115 = bf16[2,4,32,1024]{3,2,1,0:T(8,128)(2,1)S(1)} custom-call(bf16[2,4,2,2,2,32,1024]{6,5,4,3,2,1,0:T(8,128)(2,1)S(1)} %bitcast.17), custom_call_target="tpu_custom_call" | custom-call | tf_op jit(solution)/shard_map/pallas_call | solution.py:607
  132.0 0.1 convert_bitcast_fusion
  132.1 0.1 fusion
  132.2 0.3 copy.15
  132.6 1.0 squeeze.7
  133.5 0.3 copy.14
  133.9 1.0 squeeze.6
  (5 shorter events, 0.1 us)
Async XLA Ops:
  0.6 2.6 %copy-start = (f32[128,1024]{1,0:T(8,128)S(1)}, f32[128,1024]{1,0:T(8,128)}, u32[]{:S(2)}) copy-start(f32[128,1024]{1,0:T(8,128)} %param.12) | copy-start | bytes 1572868
  83.8 2.2 %copy-start.1 = (bf16[2,4,256,1024]{3,2,1,0:T(8,128)(2,1)S(1)}, bf16[2,4,256,1024]{3,2,1,0:T(8,128)(2,1)}, u32[]{:S(2)}) copy-start(bf16[2,4,256,1024]{3,2,1,0:T(8,128)(2,1)} %shard_map.114) | copy-start | bytes 12582916

commit v3 on v2

--- a/solution.py
+++ b/solution.py
@@ -45,7 +45,8 @@
     cent_ref,
     weight_ref,
     spec_ref,
-    narrow_ref,
+    cos_ref,
+    sin_ref,
     wide_ref,
     back_ref,
     target_ref,
@@ -57,6 +58,10 @@
     grad_ref,
     product_ref,
     scale_ref,
+    narrow_ref,
+    aim_ref,
+    own_ref,
+    own_sem,
 ):
     slots = LANES // own_rows
     quarter = spec_ref.shape[1] // RADIX
@@ -99,6 +104,34 @@
 
     lax.fori_loop(0, total_points, place_weight, 0)
 
+    if own_rows % 16 == 0:
+        first_own = pl.multiple_of(lax.axis_index("src") * own_rows, own_rows)
+        first_row = lax.axis_index("row") * target_ref.shape[0] + first_own
+        own = pl.ds(pl.multiple_of(first_row, own_rows), own_rows)
+        copies = [
+            pltpu.make_async_copy(table.at[own, :], own_ref.at[part], own_sem.at[part])
+            for part, table in enumerate((cos_ref, sin_ref))
+        ]
+        for copy in copies:
+            copy.start()
+        aim = jnp.concatenate([target_ref[pl.ds(first_own, own_rows), :]] * slots, axis=0).T
+        for copy in copies:
+            copy.wait()
+        for slot in range(slots):
+            low = pl.ds(slot * own_rows, own_rows)
+            high = pl.ds(LANES + slot * own_rows, own_rows)
+            narrow_ref[0, low, :] = own_ref[0]
+            narrow_ref[0, high, :] = own_ref[1]
+            narrow_ref[1, low, :] = -own_ref[1]
+            narrow_ref[1, high, :] = own_ref[0]
+    else:
+        aim = target_ref[...]
+        narrow_ref[0, :LANES, :] = cos_ref[...]
+        narrow_ref[0, LANES:, :] = sin_ref[...]
+        narrow_ref[1, :LANES, :] = -sin_ref[...]
+        narrow_ref[1, LANES:, :] = cos_ref[...]
+    aim_ref[...] = aim.reshape(aim_ref.shape)
+
     band_ref[...] = jnp.zeros_like(band_ref)
     grad_ref[...] = jnp.zeros_like(grad_ref)
 
@@ -134,7 +167,7 @@
             band_ref[residue, rows_i, high] += real
         return carry
 
-    lax.fori_loop(0, total_points, spread, 0)
+    lax.fori_loop(0, total_points, spread, 0, unroll=4)
 
     power_ref[...] = jnp.zeros_like(power_ref)
 
@@ -157,7 +190,7 @@
             power_ref[index] += weight * (real * real + imag * imag)
         return carry
 
-    lax.fori_loop(0, groups, forward, 0)
+    lax.fori_loop(0, groups, forward, 0, unroll=2)
 
     for index in range(RADIX):
         power = power_ref[index]
@@ -165,7 +198,7 @@
         while shift < LANES:
             power = power + pltpu.roll(power, shift, 1)
             shift *= 2
-        power_ref[index] = power * (2.0 / total_points) - 2.0 * target_ref[index]
+        power_ref[index] = power * (2.0 / total_points) - 2.0 * aim_ref[index]
 
     def backward(group, carry):
         base = pl.multiple_of(group * (2 * LANES), 2 * LANES)
@@ -194,7 +227,7 @@
             ).astype(jnp.bfloat16)
         return carry
 
-    lax.fori_loop(0, groups, backward, 0)
+    lax.fori_loop(0, groups, backward, 0, unroll=2)
 
     def collect(point, carry):
         first_q, first_l, masks = window(point, True)
@@ -215,7 +248,7 @@
                 grad_ref[where] += jnp.where(mask, piece, 0.0)
         return carry
 
-    lax.fori_loop(0, total_points, collect, 0)
+    lax.fori_loop(0, total_points, collect, 0, unroll=4)
     out_ref[...] = grad_ref[...].astype(out_ref.dtype)
 
 
@@ -245,11 +278,14 @@
     sources,
     re_ref,
     im_ref,
-    cent_ref,
-    weight_ref,
+    cent_row_ref,
+    cent_col_ref,
+    weight_row_ref,
     spec_ref,
     cents_ref,
     weights_ref,
+    cent_ref,
+    weight_ref,
     local_sem,
     send_sem,
     recv_sem,
@@ -262,6 +298,12 @@
     rows_dev = re_ref.shape[0]
     own = lax.axis_index("src")
     peers = [(own + step) % sources for step in range(1, sources)]
+    points_dev = weight_row_ref.shape[1]
+    cent_ref[...] = jnp.zeros_like(cent_ref)
+    weight_ref[...] = jnp.zeros_like(weight_ref)
+    cent_ref[0:1, 0:points_dev] = cent_row_ref[...]
+    cent_ref[1:2, 0:points_dev] = cent_col_ref[...]
+    weight_ref[0:1, 0:points_dev] = weight_row_ref[...]
     enter([mate, across_x, across_y], peers)
 
     def rows_of(device):
@@ -290,9 +332,6 @@
                     device_id_type=pl.DeviceIdType.MESH,
                 )
             )
-    for copy in small:
-        copy.start()
-
     sent = []
 
     def send(part, holder, to):
@@ -315,6 +354,8 @@
     im_y = send(1, None, across_y)
     im_x = send(1, None, across_x)
     re_y = send(0, None, across_y)
+    for copy in small:
+        copy.start()
     send(0, None, mate)
     send(1, None, mate)
     re_x.wait_recv()
@@ -346,7 +387,11 @@
 def reduce_kernel(
     sources,
     part_ref,
-    out_ref,
+    out_re_ref,
+    out_im_ref,
+    plane,
+    own_part,
+    own_sem,
     mate_in,
     chip_sum,
     first_re_in,
@@ -368,7 +413,9 @@
     down_recv,
 ):
     row, core, x, y, mate, across_x, across_y = row_place()
-    chunks = part_ref.shape[1]
+    chunks = mate_in.shape[0]
+    width = mate_in.shape[-1]
+    halves = chunks // part_ref.shape[1]
     own = lax.axis_index("src")
     root = sources // 2
     has_left = jnp.logical_and(own > 0, own <= root)
@@ -398,15 +445,33 @@
         )
 
     pair, step_re, step_im, end_re, end_im = {}, {}, {}, {}, {}
+    keep = {}
     for chunk in range(chunks):
+        residue = chunk // halves
+        cols = pl.ds(chunk % halves * width, width)
         pair[chunk] = row_copy(
-            0, chunk, part_ref.at[:, chunk, :, :, 1 - core], mate_in.at[chunk], mate
+            0, chunk, part_ref.at[:, residue, :, :, 1 - core, :, cols], mate_in.at[chunk], mate
         )
         pair[chunk].start()
+        keep[chunk] = pltpu.make_async_copy(
+            part_ref.at[:, residue, :, :, core, :, cols], own_part.at[chunk], own_sem.at[chunk]
+        )
+        keep[chunk].start()
+
+    def place(chunk, source):
+        residue = chunk // halves
+        blocks = width // LANES
+        rows = pl.ds(residue, source.shape[2], stride=RADIX)
+        for part in range(2):
+            for block in range(blocks):
+                plane[part, chunk % halves * blocks + block, rows, :] = wide(
+                    source[chunk, part, :, block * LANES : (block + 1) * LANES]
+                )
 
     def add_pair(chunk):
+        keep[chunk].wait()
         pair[chunk].wait_recv()
-        total = wide(part_ref[:, chunk, :, :, core]) + wide(mate_in[chunk])
+        total = wide(own_part[chunk]) + wide(mate_in[chunk])
         chip_sum[chunk] = total.astype(chip_sum.dtype)
         step_re[chunk] = row_copy(
             1, chunk, chip_sum.at[chunk, 0, :, 1 - x], first_re_in.at[chunk], across_x
@@ -506,7 +571,7 @@
                 down_left(chunk, chain).start()
             if root < sources - 1:
                 down_right(chunk, chain).start()
-            out_ref[:, chunk] = chain[chunk]
+            place(chunk, chain)
 
     def spread_final(chunk):
         @pl.when(own < root)
@@ -517,7 +582,7 @@
             def _():
                 down_left(chunk, final_in).start()
 
-            out_ref[:, chunk] = final_in[chunk]
+            place(chunk, final_in)
 
         @pl.when(own > root)
         def _():
@@ -527,7 +592,7 @@
             def _():
                 down_right(chunk, final_in).start()
 
-            out_ref[:, chunk] = final_in[chunk]
+            place(chunk, final_in)
 
     stages = ((add_pair, 0), (add_first, 1), (add_last, 2), (spread_final, 4))
     for time in range(chunks + 4):
@@ -535,6 +600,10 @@
             if 0 <= time - lag < chunks:
                 stage(time - lag)
 
+    for part, out_ref in enumerate((out_re_ref, out_im_ref)):
+        for block in range(plane.shape[1]):
+            out_ref[:, block * LANES : (block + 1) * LANES] = plane[part, block]
+
     for chunk in range(chunks):
         for group in (pair, step_re, step_im, end_re, end_im):
             group[chunk].wait_send()
@@ -563,11 +632,16 @@
                 down_right(chunk, chain).wait_send()
 
 
-def gather_all(spec_re, spec_im, cents, weights, sources, kernels):
+def gather_all(spec_re, spec_im, cent_row, cent_col, weights, sources, kernels):
     rows_dev, band = spec_re.shape
+    points_dev = weights.shape[0]
     if not kernels:
+        pad = ((0, 6), (0, LANES - points_dev))
+        cents = jnp.pad(jnp.stack([cent_row, cent_col], axis=0), pad)
+        weights = jnp.pad(jnp.stack([weights, weights], axis=0), pad)
         spectrum = lax.all_gather(jnp.stack([spec_re, spec_im]), "row", axis=1, tiled=True)
         return spectrum, lax.all_gather(cents, "src"), lax.all_gather(weights, "src")
+    tile = (8, LANES)
     hbm = pl.BlockSpec(memory_space=pl.ANY)
     vmem = pl.BlockSpec(memory_space=pltpu.VMEM)
     dma = pltpu.SemaphoreType.DMA
@@ -575,12 +649,14 @@
         functools.partial(gather_kernel, sources),
         out_shape=(
             jax.ShapeDtypeStruct((2, rows_dev * lax.axis_size("row"), band), spec_re.dtype),
-            jax.ShapeDtypeStruct((sources,) + cents.shape, cents.dtype),
-            jax.ShapeDtypeStruct((sources,) + weights.shape, weights.dtype),
+            jax.ShapeDtypeStruct((sources,) + tile, cent_row.dtype),
+            jax.ShapeDtypeStruct((sources,) + tile, weights.dtype),
         ),
-        in_specs=[hbm, hbm, vmem, vmem],
+        in_specs=[hbm, hbm, vmem, vmem, vmem],
         out_specs=(hbm, vmem, vmem),
         scratch_shapes=[
+            pltpu.VMEM(tile, cent_row.dtype),
+            pltpu.VMEM(tile, weights.dtype),
             dma((4,)),
             dma((14,)),
             dma((14,)),
@@ -588,28 +664,37 @@
             dma((2, max(sources - 1, 1))),
         ],
         compiler_params=pltpu.CompilerParams(collective_id=0, has_side_effects=True),
-    )(spec_re, spec_im, cents, weights)
+    )(spec_re, spec_im, cent_row[None], cent_col[None], weights[None])
 
 
 def reduce_all(partial, sources, kernels):
     _, residues, quarter, band = partial.shape
+    own = quarter // lax.axis_size("row")
+    rows_dev = own * residues
     if not kernels:
         summed = lax.psum_scatter(partial, "row", scatter_dimension=2, tiled=True)
-        return lax.psum(summed, "src")
-    own = quarter // lax.axis_size("row")
+        summed = lax.psum(summed, "src").astype(jnp.float32)
+        summed = summed.transpose(0, 2, 1, 3).reshape(2, rows_dev, band)
+        return summed[0], summed[1]
+    halves = 2
+    chunks = residues * halves
     partial = partial.reshape(2, residues, 2, 2, 2, own, band)
     vmem = pl.BlockSpec(memory_space=pltpu.VMEM)
     dma = pltpu.SemaphoreType.DMA
 
     def buffer(*lead):
-        return pltpu.VMEM((residues,) + lead + (own, band), partial.dtype)
-
+        return pltpu.VMEM((chunks,) + lead + (own, band // halves), partial.dtype)
+
+    result = jax.ShapeDtypeStruct((rows_dev, band), jnp.float32)
     return pl.pallas_call(
         functools.partial(reduce_kernel, sources),
-        out_shape=jax.ShapeDtypeStruct((2, residues, own, band), partial.dtype),
-        in_specs=[vmem],
-        out_specs=vmem,
+        out_shape=(result, result),
+        in_specs=[pl.BlockSpec(memory_space=pl.ANY)],
+        out_specs=(vmem, vmem),
         scratch_shapes=[
+            pltpu.VMEM((2, band // LANES, rows_dev, LANES), jnp.float32),
+            buffer(2, 2, 2),
+            dma((chunks,)),
             buffer(2, 2, 2),
             buffer(2, 2, 2),
             buffer(2),
@@ -622,13 +707,13 @@
             buffer(2),
             buffer(2),
             buffer(2),
-            dma((5, residues)),
-            dma((5, residues)),
-            dma((residues,)),
-            dma((residues,)),
-            dma((residues,)),
-            dma((2, residues)),
-            dma((residues,)),
+            dma((5, chunks)),
+            dma((5, chunks)),
+            dma((chunks,)),
+            dma((chunks,)),
+            dma((chunks,)),
+            dma((2, chunks)),
+            dma((chunks,)),
         ],
         compiler_params=pltpu.CompilerParams(
             collective_id=1, has_side_effects=True, vmem_limit_bytes=40 * 1024 * 1024
@@ -648,42 +733,35 @@
     cosine, sine = host_tables(band)
 
     kernels = lax.axis_size("row") == 8 and rows_dev % (RADIX * 16) == 0
-    cents = jnp.stack([cent_row, cent_col], axis=0)
-    cents = jnp.pad(cents, ((0, 6), (0, LANES - points_dev)))
-    weights_wide = jnp.pad(weights[None], ((0, 7), (0, LANES - points_dev)))
     spectrum, cents_all, weights_all = gather_all(
-        spec_re, spec_im, cents, weights_wide, groups_src, kernels
+        spec_re, spec_im, cent_row, cent_col, weights, groups_src, kernels
     )
 
-    first_own = lax.axis_index("src") * own_rows
-    first_row = lax.axis_index("row") * target.shape[0] + first_own
-    cos_own = lax.dynamic_slice_in_dim(jnp.asarray(cosine), first_row, own_rows, 0)
-    sin_own = lax.dynamic_slice_in_dim(jnp.asarray(sine), first_row, own_rows, 0)
-    cos_many = jnp.tile(cos_own, (slots, 1))
-    sin_many = jnp.tile(sin_own, (slots, 1))
-    narrow = jnp.stack(
-        [
-            jnp.concatenate([cos_many, sin_many], axis=0),
-            jnp.concatenate([-sin_many, cos_many], axis=0),
-        ],
-        axis=0,
-    )
+    cos_own, sin_own, target_own = jnp.asarray(cosine), jnp.asarray(sine), target
+    if own_rows % 16:
+        first_own = lax.axis_index("src") * own_rows
+        first_row = lax.axis_index("row") * target.shape[0] + first_own
+        cos_own = lax.dynamic_slice_in_dim(cos_own, first_row, own_rows, 0)
+        sin_own = lax.dynamic_slice_in_dim(sin_own, first_row, own_rows, 0)
+        cos_own = jnp.tile(cos_own, (slots, 1))
+        sin_own = jnp.tile(sin_own, (slots, 1))
+        target_own = lax.dynamic_slice_in_dim(target, first_own, own_rows, 0)
+        target_own = jnp.tile(target_own, (slots, 1)).T
     cos_split = cosine[:quarter].reshape(quarter, quarter, RADIX).transpose(2, 0, 1)
     sin_split = sine[:quarter].reshape(quarter, quarter, RADIX).transpose(2, 0, 1)
     wide = jnp.asarray(np.concatenate([cos_split, sin_split], axis=2))
     back = jnp.asarray(
         np.concatenate([cos_split.transpose(0, 2, 1), sin_split.transpose(0, 2, 1)], axis=2)
     )
-    target_own = lax.dynamic_slice_in_dim(target, first_own, own_rows, 0)
-    target_own = jnp.tile(target_own, (slots, 1)).T.reshape(RADIX, quarter, LANES)
 
     vmem = pl.BlockSpec(memory_space=pltpu.VMEM)
+    table = vmem if own_rows % 16 else pl.BlockSpec(memory_space=pl.ANY)
     smem = pl.BlockSpec(memory_space=pltpu.SMEM)
     lanes_all = 2 * own_rows * total_points
     partial = pl.pallas_call(
         functools.partial(main_kernel, total_points, own_rows),
         out_shape=jax.ShapeDtypeStruct((2, RADIX, quarter, band), jnp.bfloat16),
-        in_specs=[smem, smem] + [vmem] * 5,
+        in_specs=[smem, smem, vmem, table, table, vmem, vmem, vmem],
         out_specs=vmem,
         scratch_shapes=[
             pltpu.VMEM((RADIX, 2 * quarter, lanes_all), jnp.bfloat16),
@@ -693,13 +771,15 @@
             pltpu.VMEM((2, RADIX, quarter, band), jnp.float32),
             pltpu.VMEM((2, RADIX * WIN_Q, LANES), jnp.float32),
             pltpu.VMEM((groups, 1, LANES), jnp.float32),
+            pltpu.VMEM((2, 2 * LANES, band), jnp.bfloat16),
+            pltpu.VMEM((RADIX, quarter, LANES), jnp.float32),
+            pltpu.VMEM((2, max(own_rows, 16), band), jnp.bfloat16),
+            pltpu.SemaphoreType.DMA((2,)),
         ],
         compiler_params=pltpu.CompilerParams(vmem_limit_bytes=56 * 1024 * 1024),
-    )(cents_all, weights_all, spectrum, narrow, wide, back, target_own)
-
-    summed = reduce_all(partial, groups_src, kernels).astype(jnp.float32)
-    summed = summed.transpose(0, 2, 1, 3).reshape(2, rows_dev, band)
-    return summed[0], summed[1]
+    )(cents_all, weights_all, spectrum, cos_own, sin_own, wide, back, target_own)
+
+    return reduce_all(partial, groups_src, kernels)
 
 
 def solution(mesh):

time: 135 us -> 139 us (1.030)
  Pallas kernels: 123 us -> 135 us
  local copies, waits for them, and re-layouts: 8.73 us -> 3.77 us
  other arithmetic: 2.12 us -> 0 us
    pallas_call x1, Pallas kernels: 46 us -> 65.9 us  [reduce_all(): pl.pallas_call(functools.partial(reduce_kernel, sources), out_shape=(resu...]
    pallas_call x1, Pallas kernels: 49.5 us -> 40.9 us  [local(): pl.pallas_call(functools.partial(main_kernel, total_points, own_rows), ou...]
    another operation x3 -> x0, other arithmetic: 1.99 us -> none  [the longest x2 1.25 us: local(): jnp.stack([jnp.concatenate([cos_many, sin_many], axis=0), jnp.concatenate...]
    squeeze x2 -> x0, local copies, waits for them, and re-layouts: 1.95 us -> none  [local(): return (summed[0], summed[1])]
    pad x2 -> x0, local copies, waits for them, and re-layouts: 1.85 us -> none  [the longest x1 1.25 us: local(): weights_wide = jnp.pad(weights[None], ((0, 7), (0, LANES - points_dev)))]
    unnamed x4, local copies, waits for them, and re-layouts: 2.2 us -> 3.77 us
where the time goes in v3:
time: 139 us
  Pallas kernels  135 us (97%)
  local copies, waits for them, and re-layouts  3.77 us (3%)
    pallas_call x1, Pallas kernels, reduce_all(): pl.pallas_call(functools.partial(reduce_kernel, sources), out_shape=(resu...  65.9 us
    pallas_call x1, Pallas kernels, local(): pl.pallas_call(functools.partial(main_kernel, total_points, own_rows), ou...  40.9 us
    pallas_call x1, Pallas kernels, gather_all(): pl.pallas_call(functools.partial(gather_kernel, sources), out_shape=(jax....  27.8 us
    unnamed x4, local copies, waits for them, and re-layouts  3.77 us

profile of v3, /device:TPU:0, one launch (start us, length us, event | category | flops | bytes accessed | tf_op | source)
XLA Modules:
  0.0 139.0 jit_solution(1706419515786465995)
XLA Ops:
  0.6 27.8 %shard_map.113 = (bf16[2,1024,1024]{2,1,0:T(8,128)(2,1)}, s32[4,8,128]{2,1,0:T(8,128)}, f32[4,8,128]{2,1,0:T(8,128)}) custom-call(bf16[128,1024]{1,0:T(8,128)(2,1)} %re_ref.1, bf16[128,1024]{1,0:T(8,128)(2,1)} %im_ref.1, s32[1,8]{1,0:T(1,128)} %bitcast.5, s32[1,8]{1,0:T(1,128)} %bitcast.6, f32[1,8]{1,0:T(1,128)} %bitcast.7), custom_call_target="tpu_custom_call" | custom-call | tf_op jit(solution)/shard_map/pallas_call | solution.py:648
  28.4 40.9 %shard_map.114 = bf16[2,4,256,1024]{3,2,1,0:T(8,128)(2,1)} custom-call(s32[4,8,128]{2,1,0:T(8,128)} %get-tuple-element.5.cent_ref, f32[4,8,128]{2,1,0:T(8,128)} %get-tuple-element.6.weight_ref, bf16[2,1024,1024]{2,1,0:T(8,128)(2,1)} %get-tuple-element.7.spec_ref, bf16[1024,1024]{1,0:T(8,128)(2,1)} %constant.8.clone.cos_ref, ...), custom_call_target="tpu_custom_call" | custom-call | tf_op jit(solution)/shard_map/pallas_call | solution.py:761
  69.3 0.0 copy-start
  69.3 2.2 %copy-done = bf16[2,4,256,1024]{3,2,1,0:T(8,128)(2,1)S(1)} copy-done((bf16[2,4,256,1024]{3,2,1,0:T(8,128)(2,1)S(1)}, bf16[2,4,256,1024]{3,2,1,0:T(8,128)(2,1)}, u32[]{:S(2)}) %copy-start) | copy-done | bytes 4194328
  71.5 65.9 %shard_map.115 = (f32[128,1024]{1,0:T(8,128)S(1)}, f32[128,1024]{1,0:T(8,128)S(1)}) custom-call(bf16[2,4,2,2,2,32,1024]{6,5,4,3,2,1,0:T(8,128)(2,1)S(1)} %bitcast.4), custom_call_target="tpu_custom_call" | custom-call | tf_op jit(solution)/shard_map/pallas_call | solution.py:689
  137.5 0.8 copy.14
  138.3 0.8 copy.15
Async XLA Ops:
  69.3 2.2 %copy-start = (bf16[2,4,256,1024]{3,2,1,0:T(8,128)(2,1)S(1)}, bf16[2,4,256,1024]{3,2,1,0:T(8,128)(2,1)}, u32[]{:S(2)}) copy-start(bf16[2,4,256,1024]{3,2,1,0:T(8,128)(2,1)} %shard_map.114) | copy-start | bytes 12582916

commit v4 on v3

--- a/solution.py
+++ b/solution.py
@@ -44,13 +44,19 @@
     own_rows,
     cent_ref,
     weight_ref,
-    spec_ref,
+    spec_hbm,
     cos_ref,
     sin_ref,
+    wide_hbm,
+    back_hbm,
+    target_ref,
+    out_hbm,
+    spec_ref,
     wide_ref,
     back_ref,
-    target_ref,
     out_ref,
+    in_sem,
+    out_sem,
     band_ref,
     field_ref,
     adj_ref,
@@ -95,6 +101,14 @@
         lane = lax.broadcasted_iota(jnp.int32, (1, LANES), 1)
         return (lane // own_rows == slot).astype(jnp.float32)
 
+    incoming = [
+        pltpu.make_async_copy(source, target, in_sem.at[index])
+        for index, (source, target) in enumerate(
+            ((spec_hbm, spec_ref), (wide_hbm, wide_ref), (back_hbm, back_ref))
+        )
+    ]
+    for copy in incoming:
+        copy.start()
     scale_ref[...] = jnp.zeros_like(scale_ref)
 
     def place_weight(point, carry):
@@ -135,39 +149,48 @@
     band_ref[...] = jnp.zeros_like(band_ref)
     grad_ref[...] = jnp.zeros_like(grad_ref)
 
-    def spread(point, carry):
-        first_q, first_l, masks = window(point, False)
-        inside = jnp.concatenate(
-            [mask.astype(jnp.float32).astype(jnp.bfloat16) for mask in masks], axis=-1
-        )
-        rows_all = pl.ds(pl.multiple_of(first_q * RADIX, 16 * RADIX), wide_rows)
-        rows = pl.ds(first_q, WIN_Q)
-        cols = pl.ds(first_l, WIN_L)
-        masked = jnp.concatenate(
-            [spec_ref[part, rows_all, cols] * inside for part in range(2)], axis=1
-        )
-        table = jnp.concatenate([narrow_ref[0, :, cols], narrow_ref[1, :, cols]], axis=1)
-        product = lax.dot_general(
-            masked, table, (((1,), (1,)), ((), ())), preferred_element_type=jnp.float32
-        )
-        product_ref[0] = product[:, :LANES]
-        product_ref[1] = product[:, LANES:]
-        chosen = slot_lanes(point % slots)
-        base = pl.multiple_of(point // slots * (2 * LANES), 2 * LANES)
-        low = pl.ds(base, LANES)
-        high = pl.ds(base + LANES, LANES)
-        rows_i = pl.ds(quarter + first_q, WIN_Q)
-        for residue in range(RADIX):
-            picked = pl.ds(residue, WIN_Q, stride=RADIX)
-            real = (product_ref[0, picked, :] * chosen).astype(jnp.bfloat16)
-            imag = (product_ref[1, picked, :] * chosen).astype(jnp.bfloat16)
-            band_ref[residue, rows, low] += real
-            band_ref[residue, rows, high] += imag
-            band_ref[residue, rows_i, low] -= imag
-            band_ref[residue, rows_i, high] += real
+    incoming[0].wait()
+    buffers = product_ref.shape[0]
+
+    def spread(step, carry):
+        places = []
+        for buffer in range(buffers):
+            point = step * buffers + buffer
+            first_q, first_l, masks = window(point, False)
+            inside = jnp.concatenate(
+                [mask.astype(jnp.float32).astype(jnp.bfloat16) for mask in masks], axis=-1
+            )
+            rows_all = pl.ds(pl.multiple_of(first_q * RADIX, 16 * RADIX), wide_rows)
+            cols = pl.ds(first_l, WIN_L)
+            masked = jnp.concatenate(
+                [spec_ref[part, rows_all, cols] * inside for part in range(2)], axis=1
+            )
+            table = jnp.concatenate([narrow_ref[0, :, cols], narrow_ref[1, :, cols]], axis=1)
+            product = lax.dot_general(
+                masked, table, (((1,), (1,)), ((), ())), preferred_element_type=jnp.float32
+            )
+            product_ref[buffer, 0] = product[:, :LANES]
+            product_ref[buffer, 1] = product[:, LANES:]
+            places.append((point, first_q))
+        for buffer, (point, first_q) in enumerate(places):
+            chosen = slot_lanes(point % slots)
+            base = pl.multiple_of(point // slots * (2 * LANES), 2 * LANES)
+            low = pl.ds(base, LANES)
+            high = pl.ds(base + LANES, LANES)
+            rows = pl.ds(first_q, WIN_Q)
+            rows_i = pl.ds(quarter + first_q, WIN_Q)
+            for residue in range(RADIX):
+                picked = pl.ds(residue, WIN_Q, stride=RADIX)
+                real = (product_ref[buffer, 0, picked, :] * chosen).astype(jnp.bfloat16)
+                imag = (product_ref[buffer, 1, picked, :] * chosen).astype(jnp.bfloat16)
+                band_ref[residue, rows, low] += real
+                band_ref[residue, rows, high] += imag
+                band_ref[residue, rows_i, low] -= imag
+                band_ref[residue, rows_i, high] += real
         return carry
 
-    lax.fori_loop(0, total_points, spread, 0, unroll=4)
+    lax.fori_loop(0, total_points // buffers, spread, 0)
+    incoming[1].wait()
 
     power_ref[...] = jnp.zeros_like(power_ref)
 
@@ -199,6 +222,8 @@
             power = power + pltpu.roll(power, shift, 1)
             shift *= 2
         power_ref[index] = power * (2.0 / total_points) - 2.0 * aim_ref[index]
+
+    incoming[2].wait()
 
     def backward(group, carry):
         base = pl.multiple_of(group * (2 * LANES), 2 * LANES)
@@ -249,7 +274,17 @@
         return carry
 
     lax.fori_loop(0, total_points, collect, 0, unroll=4)
-    out_ref[...] = grad_ref[...].astype(out_ref.dtype)
+    leaving = []
+    for part in range(2):
+        for residue in range(RADIX):
+            out_ref[part, residue] = grad_ref[part, residue].astype(out_ref.dtype)
+            copy = pltpu.make_async_copy(
+                out_ref.at[part, residue], out_hbm.at[part, residue], out_sem.at[part, residue]
+            )
+            copy.start()
+            leaving.append(copy)
+    for copy in leaving:
+        copy.wait()
 
 
 def row_place():
@@ -306,8 +341,17 @@
     weight_ref[0:1, 0:points_dev] = weight_row_ref[...]
     enter([mate, across_x, across_y], peers)
 
-    def rows_of(device):
-        return pl.ds(pl.multiple_of(device * rows_dev, rows_dev), rows_dev)
+    parity = own % 2
+    partner = own + 1 - 2 * parity
+    few = rows_dev * 3 // 8
+    most = rows_dev - few
+    fetched = (few * parity, most)
+    passed = (most * parity, few)
+    missing = (most * (1 - parity), few)
+    whole = (0, rows_dev)
+
+    def rows_of(device, piece=whole):
+        return pl.ds(pl.multiple_of(device * rows_dev + piece[0], 16), piece[1])
 
     keep = [
         pltpu.make_async_copy(re_ref, spec_ref.at[0, rows_of(row), :], local_sem.at[0]),
@@ -334,48 +378,57 @@
             )
     sent = []
 
-    def send(part, holder, to):
-        first = holder is None
-        target = spec_ref.at[part, rows_of(row if first else holder), :]
+    def send(part, holder, piece, axis, to):
+        target = spec_ref.at[part, rows_of(row if holder is None else holder, piece), :]
+        source = target
+        if holder is None:
+            first = pl.multiple_of(piece[0], 16)
+            source = (re_ref, im_ref)[part].at[pl.ds(first, piece[1]), :]
         index = len(sent)
         copy = pltpu.make_async_remote_copy(
-            src_ref=(re_ref, im_ref)[part] if first else target,
+            src_ref=source,
             dst_ref=target,
             send_sem=send_sem.at[index],
             recv_sem=recv_sem.at[index],
-            device_id={"row": to},
+            device_id={axis: to},
             device_id_type=pl.DeviceIdType.MESH,
         )
         copy.start()
         sent.append(copy)
         return copy
 
-    re_x = send(0, None, across_x)
-    im_y = send(1, None, across_y)
-    im_x = send(1, None, across_x)
-    re_y = send(0, None, across_y)
+    re_x = send(0, None, fetched, "row", across_x)
+    im_y = send(1, None, fetched, "row", across_y)
+    im_x = send(1, None, fetched, "row", across_x)
+    re_y = send(0, None, fetched, "row", across_y)
     for copy in small:
         copy.start()
-    send(0, None, mate)
-    send(1, None, mate)
+    late = [send(part, None, whole, "row", mate) for part in range(2)]
+    partner_copies = []
+
+    def pass_on(part, holder):
+        partner_copies.append((send(part, holder, passed, "src", partner), part, holder))
+        late.append(send(part, holder, fetched, "row", mate))
+
     re_x.wait_recv()
-    re_corner = send(0, across_x, across_y)
-    send(0, across_x, mate)
+    re_corner = send(0, across_x, fetched, "row", across_y)
+    pass_on(0, across_x)
     im_y.wait_recv()
-    im_corner = send(1, across_y, across_x)
-    send(1, across_y, mate)
+    im_corner = send(1, across_y, fetched, "row", across_x)
+    pass_on(1, across_y)
     im_x.wait_recv()
-    send(1, across_x, mate)
+    pass_on(1, across_x)
     re_y.wait_recv()
-    send(0, across_y, mate)
+    pass_on(0, across_y)
     re_corner.wait_recv()
-    send(0, corner, mate)
+    pass_on(0, corner)
     im_corner.wait_recv()
-    send(1, corner, mate)
-    direct = (re_x, im_y, im_x, re_y, re_corner, im_corner)
-    for copy in sent:
-        if not any(copy is other for other in direct):
-            copy.wait_recv()
+    pass_on(1, corner)
+    for copy, part, holder in partner_copies:
+        copy.wait_recv()
+        late.append(send(part, holder, missing, "row", mate))
+    for copy in late:
+        copy.wait_recv()
     for copy in sent:
         copy.wait_send()
     for copy in small:
@@ -414,10 +467,11 @@
 ):
     row, core, x, y, mate, across_x, across_y = row_place()
     chunks = mate_in.shape[0]
-    width = mate_in.shape[-1]
+    depth = mate_in.shape[-2]
     halves = chunks // part_ref.shape[1]
     own = lax.axis_index("src")
     root = sources // 2
+    leaf = jnp.logical_or(own == 0, own == sources - 1)
     has_left = jnp.logical_and(own > 0, own <= root)
     has_right = jnp.logical_and(own >= root, own < sources - 1)
     peers = [(own + step) % sources for step in range(1, sources)]
@@ -448,23 +502,23 @@
     keep = {}
     for chunk in range(chunks):
         residue = chunk // halves
-        cols = pl.ds(chunk % halves * width, width)
+        rows = pl.ds(chunk % halves * depth, depth)
         pair[chunk] = row_copy(
-            0, chunk, part_ref.at[:, residue, :, :, 1 - core, :, cols], mate_in.at[chunk], mate
+            0, chunk, part_ref.at[:, residue, :, :, 1 - core, rows], mate_in.at[chunk], mate
         )
         pair[chunk].start()
         keep[chunk] = pltpu.make_async_copy(
-            part_ref.at[:, residue, :, :, core, :, cols], own_part.at[chunk], own_sem.at[chunk]
+            part_ref.at[:, residue, :, :, core, rows], own_part.at[chunk], own_sem.at[chunk]
         )
         keep[chunk].start()
 
     def place(chunk, source):
         residue = chunk // halves
-        blocks = width // LANES
-        rows = pl.ds(residue, source.shape[2], stride=RADIX)
+        first = residue + chunk % halves * depth * RADIX
+        rows = pl.ds(first, depth, stride=RADIX)
         for part in range(2):
-            for block in range(blocks):
-                plane[part, chunk % halves * blocks + block, rows, :] = wide(
+            for block in range(plane.shape[1]):
+                plane[part, block, rows, :] = wide(
                     source[chunk, part, :, block * LANES : (block + 1) * LANES]
                 )
 
@@ -573,32 +627,30 @@
                 down_right(chunk, chain).start()
             place(chunk, chain)
 
-    def spread_final(chunk):
-        @pl.when(own < root)
+    def pass_final(chunk):
+        @pl.when(jnp.logical_and(own < root, own > 0))
         def _():
             down_left(chunk, final_in).wait_recv()
-
-            @pl.when(own > 0)
-            def _():
-                down_left(chunk, final_in).start()
-
+            down_left(chunk, final_in).start()
             place(chunk, final_in)
 
-        @pl.when(own > root)
+        @pl.when(jnp.logical_and(own > root, own < sources - 1))
         def _():
             down_right(chunk, final_in).wait_recv()
-
-            @pl.when(own < sources - 1)
-            def _():
-                down_right(chunk, final_in).start()
-
+            down_right(chunk, final_in).start()
             place(chunk, final_in)
 
-    stages = ((add_pair, 0), (add_first, 1), (add_last, 2), (spread_final, 4))
-    for time in range(chunks + 4):
+    stages = ((add_pair, 0), (add_first, 1), (add_last, 2), (pass_final, 5))
+    for time in range(chunks + 5):
         for stage, lag in stages:
             if 0 <= time - lag < chunks:
                 stage(time - lag)
+    for chunk in range(chunks):
+
+        @pl.when(jnp.logical_and(leaf, own != root))
+        def _():
+            down_left(chunk, final_in).wait_recv()
+            place(chunk, final_in)
 
     for part, out_ref in enumerate((out_re_ref, out_im_ref)):
         for block in range(plane.shape[1]):
@@ -658,8 +710,8 @@
             pltpu.VMEM(tile, cent_row.dtype),
             pltpu.VMEM(tile, weights.dtype),
             dma((4,)),
-            dma((14,)),
-            dma((14,)),
+            dma((26,)),
+            dma((26,)),
             dma((2, max(sources - 1, 1))),
             dma((2, max(sources - 1, 1))),
         ],
@@ -683,7 +735,7 @@
     dma = pltpu.SemaphoreType.DMA
 
     def buffer(*lead):
-        return pltpu.VMEM((chunks,) + lead + (own, band // halves), partial.dtype)
+        return pltpu.VMEM((chunks,) + lead + (own // halves, band), partial.dtype)
 
     result = jax.ShapeDtypeStruct((rows_dev, band), jnp.float32)
     return pl.pallas_call(
@@ -716,7 +768,7 @@
             dma((chunks,)),
         ],
         compiler_params=pltpu.CompilerParams(
-            collective_id=1, has_side_effects=True, vmem_limit_bytes=40 * 1024 * 1024
+            collective_id=1, has_side_effects=True, vmem_limit_bytes=61 * 1024 * 1024
         ),
     )(partial)
 
@@ -732,7 +784,7 @@
     quarter = band // RADIX
     cosine, sine = host_tables(band)
 
-    kernels = lax.axis_size("row") == 8 and rows_dev % (RADIX * 16) == 0
+    kernels = lax.axis_size("row") == 8 and groups_src % 2 == 0 and rows_dev % LANES == 0
     spectrum, cents_all, weights_all = gather_all(
         spec_re, spec_im, cent_row, cent_col, weights, groups_src, kernels
     )
@@ -755,21 +807,28 @@
     )
 
     vmem = pl.BlockSpec(memory_space=pltpu.VMEM)
-    table = vmem if own_rows % 16 else pl.BlockSpec(memory_space=pl.ANY)
+    hbm = pl.BlockSpec(memory_space=pl.ANY)
+    table = vmem if own_rows % 16 else hbm
     smem = pl.BlockSpec(memory_space=pltpu.SMEM)
     lanes_all = 2 * own_rows * total_points
     partial = pl.pallas_call(
         functools.partial(main_kernel, total_points, own_rows),
         out_shape=jax.ShapeDtypeStruct((2, RADIX, quarter, band), jnp.bfloat16),
-        in_specs=[smem, smem, vmem, table, table, vmem, vmem, vmem],
-        out_specs=vmem,
+        in_specs=[smem, smem, hbm, table, table, hbm, hbm, vmem],
+        out_specs=hbm,
         scratch_shapes=[
+            pltpu.VMEM(spectrum.shape, spectrum.dtype),
+            pltpu.VMEM(wide.shape, wide.dtype),
+            pltpu.VMEM(back.shape, back.dtype),
+            pltpu.VMEM((2, RADIX, quarter, band), jnp.bfloat16),
+            pltpu.SemaphoreType.DMA((3,)),
+            pltpu.SemaphoreType.DMA((2, RADIX)),
             pltpu.VMEM((RADIX, 2 * quarter, lanes_all), jnp.bfloat16),
             pltpu.VMEM((RADIX, quarter, lanes_all), jnp.float32),
             pltpu.VMEM((RADIX, quarter, lanes_all), jnp.bfloat16),
             pltpu.VMEM((RADIX, quarter, LANES), jnp.float32),
             pltpu.VMEM((2, RADIX, quarter, band), jnp.float32),
-            pltpu.VMEM((2, RADIX * WIN_Q, LANES), jnp.float32),
+            pltpu.VMEM((4, 2, RADIX * WIN_Q, LANES), jnp.float32),
             pltpu.VMEM((groups, 1, LANES), jnp.float32),
             pltpu.VMEM((2, 2 * LANES, band), jnp.bfloat16),
             pltpu.VMEM((RADIX, quarter, LANES), jnp.float32),

time: 139 us -> 115 us (0.83)
  Pallas kernels: 135 us -> 110 us
    pallas_call x1, Pallas kernels: 65.9 us -> 42.3 us  [reduce_all(): pl.pallas_call(functools.partial(reduce_kernel, sources), out_shape=(resu...]
    unnamed x4 -> x2, local copies, waits for them, and re-layouts: 3.77 us -> 3.77 us
where the time goes in v4:
time: 115 us
  Pallas kernels  110 us (96%)
  local copies, waits for them, and re-layouts  3.77 us (3%)
    pallas_call x1, Pallas kernels, reduce_all(): pl.pallas_call(functools.partial(reduce_kernel, sources), out_shape=(resu...  42.3 us
    pallas_call x1, Pallas kernels, local(): pl.pallas_call(functools.partial(main_kernel, total_points, own_rows), ou...  39.9 us
    pallas_call x1, Pallas kernels, gather_all(): pl.pallas_call(functools.partial(gather_kernel, sources), out_shape=(jax....  28.1 us
    unnamed x2, local copies, waits for them, and re-layouts  3.77 us

profile of v4, /device:TPU:0, one launch (start us, length us, event | category | flops | bytes accessed | tf_op | source)
XLA Modules:
  0.0 114.8 jit_solution(517990859865836240)
XLA Ops:
  0.6 28.1 %shard_map.113 = (bf16[2,1024,1024]{2,1,0:T(8,128)(2,1)}, s32[4,8,128]{2,1,0:T(8,128)}, f32[4,8,128]{2,1,0:T(8,128)}) custom-call(bf16[128,1024]{1,0:T(8,128)(2,1)} %re_ref.1, bf16[128,1024]{1,0:T(8,128)(2,1)} %im_ref.1, s32[1,8]{1,0:T(1,128)} %bitcast.5, s32[1,8]{1,0:T(1,128)} %bitcast.6, f32[1,8]{1,0:T(1,128)} %bitcast.7), custom_call_target="tpu_custom_call" | custom-call | tf_op jit(solution)/shard_map/pallas_call | solution.py:700
  28.8 39.9 %shard_map.114 = bf16[2,4,256,1024]{3,2,1,0:T(8,128)(2,1)} custom-call(s32[4,8,128]{2,1,0:T(8,128)} %get-tuple-element.5.cent_ref, f32[4,8,128]{2,1,0:T(8,128)} %get-tuple-element.6.weight_ref, bf16[2,1024,1024]{2,1,0:T(8,128)(2,1)} %get-tuple-element.7.spec_hbm, bf16[1024,1024]{1,0:T(8,128)(2,1)} %constant.8.clone.cos_ref, ...), custom_call_target="tpu_custom_call" | custom-call | tf_op jit(solution)/shard_map/pallas_call | solution.py:814
  68.7 42.3 %shard_map.115 = (f32[128,1024]{1,0:T(8,128)}, f32[128,1024]{1,0:T(8,128)}) custom-call(bf16[2,4,2,2,2,32,1024]{6,5,4,3,2,1,0:T(8,128)(2,1)} %bitcast.4), custom_call_target="tpu_custom_call" | custom-call | tf_op jit(solution)/shard_map/pallas_call | solution.py:741
  111.0 1.9 %copy.14 = f32[128,1024]{1,0:T(8,128)} copy(f32[128,1024]{1,0:T(8,128)} %get-tuple-element.10) | data formatting | bytes 1048576
  112.9 1.9 %copy.15 = f32[128,1024]{1,0:T(8,128)} copy(f32[128,1024]{1,0:T(8,128)} %get-tuple-element.11) | data formatting | bytes 1048576

commit v5 on v4

--- a/solution.py
+++ b/solution.py
@@ -65,6 +65,7 @@
     product_ref,
     scale_ref,
     narrow_ref,
+    tall_ref,
     aim_ref,
     own_ref,
     own_sem,
@@ -145,6 +146,8 @@
         narrow_ref[1, :LANES, :] = -sin_ref[...]
         narrow_ref[1, LANES:, :] = cos_ref[...]
     aim_ref[...] = aim.reshape(aim_ref.shape)
+    for part in range(2):
+        tall_ref[part] = narrow_ref[part].astype(jnp.float32).T.astype(tall_ref.dtype)
 
     band_ref[...] = jnp.zeros_like(band_ref)
     grad_ref[...] = jnp.zeros_like(grad_ref)
@@ -165,10 +168,8 @@
             masked = jnp.concatenate(
                 [spec_ref[part, rows_all, cols] * inside for part in range(2)], axis=1
             )
-            table = jnp.concatenate([narrow_ref[0, :, cols], narrow_ref[1, :, cols]], axis=1)
-            product = lax.dot_general(
-                masked, table, (((1,), (1,)), ((), ())), preferred_element_type=jnp.float32
-            )
+            table = jnp.concatenate([tall_ref[0, cols, :], tall_ref[1, cols, :]], axis=0)
+            product = jnp.dot(masked, table, preferred_element_type=jnp.float32)
             product_ref[buffer, 0] = product[:, :LANES]
             product_ref[buffer, 1] = product[:, LANES:]
             places.append((point, first_q))
@@ -440,8 +441,7 @@
 def reduce_kernel(
     sources,
     part_ref,
-    out_re_ref,
-    out_im_ref,
+    out_ref,
     plane,
     own_part,
     own_sem,
@@ -506,10 +506,12 @@
         pair[chunk] = row_copy(
             0, chunk, part_ref.at[:, residue, :, :, 1 - core, rows], mate_in.at[chunk], mate
         )
-        pair[chunk].start()
         keep[chunk] = pltpu.make_async_copy(
             part_ref.at[:, residue, :, :, core, rows], own_part.at[chunk], own_sem.at[chunk]
         )
+    ahead = 2
+    for chunk in range(ahead):
+        pair[chunk].start()
         keep[chunk].start()
 
     def place(chunk, source):
@@ -525,6 +527,9 @@
     def add_pair(chunk):
         keep[chunk].wait()
         pair[chunk].wait_recv()
+        if chunk + ahead < chunks:
+            pair[chunk + ahead].start()
+            keep[chunk + ahead].start()
         total = wide(own_part[chunk]) + wide(mate_in[chunk])
         chip_sum[chunk] = total.astype(chip_sum.dtype)
         step_re[chunk] = row_copy(
@@ -652,9 +657,10 @@
             down_left(chunk, final_in).wait_recv()
             place(chunk, final_in)
 
-    for part, out_ref in enumerate((out_re_ref, out_im_ref)):
+    for part in range(2):
         for block in range(plane.shape[1]):
-            out_ref[:, block * LANES : (block + 1) * LANES] = plane[part, block]
+            cols = slice(block * LANES, (block + 1) * LANES)
+            out_ref[part, :, cols] = plane[part, block].astype(out_ref.dtype)
 
     for chunk in range(chunks):
         for group in (pair, step_re, step_im, end_re, end_im):
@@ -737,12 +743,11 @@
     def buffer(*lead):
         return pltpu.VMEM((chunks,) + lead + (own // halves, band), partial.dtype)
 
-    result = jax.ShapeDtypeStruct((rows_dev, band), jnp.float32)
-    return pl.pallas_call(
+    summed = pl.pallas_call(
         functools.partial(reduce_kernel, sources),
-        out_shape=(result, result),
+        out_shape=jax.ShapeDtypeStruct((2, rows_dev, band), partial.dtype),
         in_specs=[pl.BlockSpec(memory_space=pl.ANY)],
-        out_specs=(vmem, vmem),
+        out_specs=vmem,
         scratch_shapes=[
             pltpu.VMEM((2, band // LANES, rows_dev, LANES), jnp.float32),
             buffer(2, 2, 2),
@@ -771,6 +776,7 @@
             collective_id=1, has_side_effects=True, vmem_limit_bytes=61 * 1024 * 1024
         ),
     )(partial)
+    return summed[0].astype(jnp.float32), summed[1].astype(jnp.float32)
 
 
 def local(spec_re, spec_im, target, weights, cent_row, cent_col):
@@ -831,6 +837,7 @@
             pltpu.VMEM((4, 2, RADIX * WIN_Q, LANES), jnp.float32),
             pltpu.VMEM((groups, 1, LANES), jnp.float32),
             pltpu.VMEM((2, 2 * LANES, band), jnp.bfloat16),
+            pltpu.VMEM((2, band, 2 * LANES), jnp.bfloat16),
             pltpu.VMEM((RADIX, quarter, LANES), jnp.float32),
             pltpu.VMEM((2, max(own_rows, 16), band), jnp.bfloat16),
             pltpu.SemaphoreType.DMA((2,)),

time: 115 us -> 113 us (0.983)
  local copies, waits for them, and re-layouts: 3.77 us -> 0 us
  other arithmetic: 0 us -> 2.11 us
    unnamed x2 -> x0, local copies, waits for them, and re-layouts: 3.77 us -> none
    convert_element_type x0 -> x1, other arithmetic: none -> 2.11 us  [reduce_all(): return (summed[0].astype(jnp.float32), summed[1].astype(jnp.float32))]
where the time goes in v5:
time: 113 us
  Pallas kernels  110 us (97%)
  other arithmetic  2.11 us (2%)
    pallas_call x1, Pallas kernels, reduce_all(): pl.pallas_call(functools.partial(reduce_kernel, sources), out_shape=jax.S...  42.3 us
    pallas_call x1, Pallas kernels, local(): pl.pallas_call(functools.partial(main_kernel, total_points, own_rows), ou...  39.6 us
    pallas_call x1, Pallas kernels, gather_all(): pl.pallas_call(functools.partial(gather_kernel, sources), out_shape=(jax....  28.1 us

profile of v5, /device:TPU:0, one launch (start us, length us, event | category | flops | bytes accessed | tf_op | source)
XLA Modules:
  0.0 112.8 jit_solution(1568740645581044471)
XLA Ops:
  0.6 28.1 %shard_map.113 = (bf16[2,1024,1024]{2,1,0:T(8,128)(2,1)}, s32[4,8,128]{2,1,0:T(8,128)}, f32[4,8,128]{2,1,0:T(8,128)}) custom-call(bf16[128,1024]{1,0:T(8,128)(2,1)} %re_ref.1, bf16[128,1024]{1,0:T(8,128)(2,1)} %im_ref.1, s32[1,8]{1,0:T(1,128)} %bitcast.11, s32[1,8]{1,0:T(1,128)} %bitcast.12, f32[1,8]{1,0:T(1,128)} %bitcast.13), custom_call_target="tpu_custom_call" | custom-call | tf_op jit(solution)/shard_map/pallas_call | solution.py:706
  28.8 39.6 %shard_map.114 = bf16[2,4,256,1024]{3,2,1,0:T(8,128)(2,1)} custom-call(s32[4,8,128]{2,1,0:T(8,128)} %get-tuple-element.5.cent_ref, f32[4,8,128]{2,1,0:T(8,128)} %get-tuple-element.6.weight_ref, bf16[2,1024,1024]{2,1,0:T(8,128)(2,1)} %get-tuple-element.7.spec_hbm, bf16[1024,1024]{1,0:T(8,128)(2,1)} %constant.8.clone.cos_ref, ...), custom_call_target="tpu_custom_call" | custom-call | tf_op jit(solution)/shard_map/pallas_call | solution.py:820
  68.4 42.3 %shard_map.115 = bf16[2,128,1024]{2,1,0:T(8,128)(2,1)} custom-call(bf16[2,4,2,2,2,32,1024]{6,5,4,3,2,1,0:T(8,128)(2,1)} %bitcast.10), custom_call_target="tpu_custom_call" | custom-call | tf_op jit(solution)/shard_map/pallas_call | solution.py:746
  110.7 2.1 %bitcast_convert_fusion = (f32[128,1024]{1,0:T(8,128)}, f32[128,1024]{1,0:T(8,128)}) fusion(bf16[2,128,1024]{2,1,0:T(8,128)(2,1)} %shard_map.115), kind=kLoop, calls=%fused_computation | loop fusion | flops 262144 | bytes 1572864 | tf_op jit(solution)/shard_map/convert_element_type | solution.py:779

commit v6 on v5

--- a/solution.py
+++ b/solution.py
@@ -117,7 +117,7 @@
         scale_ref[point // slots] += weight * slot_lanes(point % slots)
         return carry
 
-    lax.fori_loop(0, total_points, place_weight, 0)
+    lax.fori_loop(0, total_points, place_weight, 0, unroll=16)
 
     if own_rows % 16 == 0:
         first_own = pl.multiple_of(lax.axis_index("src") * own_rows, own_rows)
@@ -146,8 +146,11 @@
         narrow_ref[1, :LANES, :] = -sin_ref[...]
         narrow_ref[1, LANES:, :] = cos_ref[...]
     aim_ref[...] = aim.reshape(aim_ref.shape)
-    for part in range(2):
-        tall_ref[part] = narrow_ref[part].astype(jnp.float32).T.astype(tall_ref.dtype)
+    for block in range(2):
+        lanes = pl.ds(block * LANES, LANES)
+        turned = narrow_ref[0, lanes, :].astype(jnp.float32).T.astype(tall_ref.dtype)
+        tall_ref[0, :, lanes] = turned
+        tall_ref[1, :, pl.ds((1 - block) * LANES, LANES)] = -turned if block else turned
 
     band_ref[...] = jnp.zeros_like(band_ref)
     grad_ref[...] = jnp.zeros_like(grad_ref)
@@ -179,15 +182,12 @@
             low = pl.ds(base, LANES)
             high = pl.ds(base + LANES, LANES)
             rows = pl.ds(first_q, WIN_Q)
-            rows_i = pl.ds(quarter + first_q, WIN_Q)
             for residue in range(RADIX):
                 picked = pl.ds(residue, WIN_Q, stride=RADIX)
                 real = (product_ref[buffer, 0, picked, :] * chosen).astype(jnp.bfloat16)
                 imag = (product_ref[buffer, 1, picked, :] * chosen).astype(jnp.bfloat16)
                 band_ref[residue, rows, low] += real
                 band_ref[residue, rows, high] += imag
-                band_ref[residue, rows_i, low] -= imag
-                band_ref[residue, rows_i, high] += real
         return carry
 
     lax.fori_loop(0, total_points // buffers, spread, 0)
@@ -197,12 +197,15 @@
 
     def forward(group, carry):
         base = pl.multiple_of(group * (2 * LANES), 2 * LANES)
-        cols = pl.ds(base, 2 * LANES)
         parts = []
         for residue in range(RADIX):
-            product = jnp.dot(
-                wide_ref[residue], band_ref[residue, :, cols], preferred_element_type=jnp.float32
+            real = band_ref[residue, :, pl.ds(base, LANES)]
+            imag = band_ref[residue, :, pl.ds(base + LANES, LANES)]
+            operand = jnp.concatenate(
+                [jnp.concatenate([real, imag], axis=1), jnp.concatenate([-imag, real], axis=1)],
+                axis=0,
             )
+            product = jnp.dot(wide_ref[residue], operand, preferred_element_type=jnp.float32)
             parts.append((product[:, :LANES], product[:, LANES:]))
         even, odd = add(parts[0], parts[2]), add(parts[1], parts[3])
         even_gap, odd_gap = sub(parts[0], parts[2]), times_i(sub(parts[1], parts[3]))
@@ -214,7 +217,7 @@
             power_ref[index] += weight * (real * real + imag * imag)
         return carry
 
-    lax.fori_loop(0, groups, forward, 0, unroll=2)
+    lax.fori_loop(0, groups, forward, 0, unroll=min(groups, 4))
 
     for index in range(RADIX):
         power = power_ref[index]
@@ -253,7 +256,7 @@
             ).astype(jnp.bfloat16)
         return carry
 
-    lax.fori_loop(0, groups, backward, 0, unroll=2)
+    lax.fori_loop(0, groups, backward, 0, unroll=min(groups, 4))
 
     def collect(point, carry):
         first_q, first_l, masks = window(point, True)
@@ -829,7 +832,7 @@
             pltpu.VMEM((2, RADIX, quarter, band), jnp.bfloat16),
             pltpu.SemaphoreType.DMA((3,)),
             pltpu.SemaphoreType.DMA((2, RADIX)),
-            pltpu.VMEM((RADIX, 2 * quarter, lanes_all), jnp.bfloat16),
+            pltpu.VMEM((RADIX, quarter, lanes_all), jnp.bfloat16),
             pltpu.VMEM((RADIX, quarter, lanes_all), jnp.float32),
             pltpu.VMEM((RADIX, quarter, lanes_all), jnp.bfloat16),
             pltpu.VMEM((RADIX, quarter, LANES), jnp.float32),

time: 113 us -> 111 us (0.982)
  Pallas kernels: 110 us -> 108 us
    pallas_call x1, Pallas kernels: 39.6 us -> 37.6 us  [local(): pl.pallas_call(functools.partial(main_kernel, total_points, own_rows), ou...]
where the time goes in v6:
time: 111 us
  Pallas kernels  108 us (97%)
  other arithmetic  2.11 us (2%)
    pallas_call x1, Pallas kernels, reduce_all(): pl.pallas_call(functools.partial(reduce_kernel, sources), out_shape=jax.S...  42.1 us
    pallas_call x1, Pallas kernels, local(): pl.pallas_call(functools.partial(main_kernel, total_points, own_rows), ou...  37.6 us
    pallas_call x1, Pallas kernels, gather_all(): pl.pallas_call(functools.partial(gather_kernel, sources), out_shape=(jax....  28.1 us

profile of v6, /device:TPU:0, one launch (start us, length us, event | category | flops | bytes accessed | tf_op | source)
XLA Modules:
  0.0 110.6 jit_solution(2238903898818565119)
XLA Ops:
  0.6 28.1 %shard_map.113 = (bf16[2,1024,1024]{2,1,0:T(8,128)(2,1)}, s32[4,8,128]{2,1,0:T(8,128)}, f32[4,8,128]{2,1,0:T(8,128)}) custom-call(bf16[128,1024]{1,0:T(8,128)(2,1)} %re_ref.1, bf16[128,1024]{1,0:T(8,128)(2,1)} %im_ref.1, s32[1,8]{1,0:T(1,128)} %bitcast.11, s32[1,8]{1,0:T(1,128)} %bitcast.12, f32[1,8]{1,0:T(1,128)} %bitcast.13), custom_call_target="tpu_custom_call" | custom-call | tf_op jit(solution)/shard_map/pallas_call | solution.py:709
  28.8 37.6 %shard_map.114 = bf16[2,4,256,1024]{3,2,1,0:T(8,128)(2,1)} custom-call(s32[4,8,128]{2,1,0:T(8,128)} %get-tuple-element.5.cent_ref, f32[4,8,128]{2,1,0:T(8,128)} %get-tuple-element.6.weight_ref, bf16[2,1024,1024]{2,1,0:T(8,128)(2,1)} %get-tuple-element.7.spec_hbm, bf16[1024,1024]{1,0:T(8,128)(2,1)} %constant.8.clone.cos_ref, ...), custom_call_target="tpu_custom_call" | custom-call | tf_op jit(solution)/shard_map/pallas_call | solution.py:823
  66.4 42.1 %shard_map.115 = bf16[2,128,1024]{2,1,0:T(8,128)(2,1)} custom-call(bf16[2,4,2,2,2,32,1024]{6,5,4,3,2,1,0:T(8,128)(2,1)} %bitcast.10), custom_call_target="tpu_custom_call" | custom-call | tf_op jit(solution)/shard_map/pallas_call | solution.py:749
  108.5 2.1 %bitcast_convert_fusion = (f32[128,1024]{1,0:T(8,128)}, f32[128,1024]{1,0:T(8,128)}) fusion(bf16[2,128,1024]{2,1,0:T(8,128)(2,1)} %shard_map.115), kind=kLoop, calls=%fused_computation | loop fusion | flops 262144 | bytes 1572864 | tf_op jit(solution)/shard_map/convert_element_type | solution.py:782

commit v7 on v6

--- a/solution.py
+++ b/solution.py
@@ -512,7 +512,7 @@
         keep[chunk] = pltpu.make_async_copy(
             part_ref.at[:, residue, :, :, core, rows], own_part.at[chunk], own_sem.at[chunk]
         )
-    ahead = 2
+    ahead = 3
     for chunk in range(ahead):
         pair[chunk].start()
         keep[chunk].start()
@@ -648,8 +648,8 @@
             down_right(chunk, final_in).start()
             place(chunk, final_in)
 
-    stages = ((add_pair, 0), (add_first, 1), (add_last, 2), (pass_final, 5))
-    for time in range(chunks + 5):
+    stages = ((add_pair, 0), (add_first, 2), (add_last, 4), (pass_final, 7))
+    for time in range(chunks + 7):
         for stage, lag in stages:
             if 0 <= time - lag < chunks:
                 stage(time - lag)

time: 111 us -> 109 us (0.982)
  Pallas kernels: 108 us -> 106 us
    pallas_call x1, Pallas kernels: 42.1 us -> 40.1 us  [reduce_all(): pl.pallas_call(functools.partial(reduce_kernel, sources), out_shape=jax.S...]
where the time goes in v7:
time: 109 us
  Pallas kernels  106 us (97%)
  other arithmetic  2.11 us (2%)
    pallas_call x1, Pallas kernels, reduce_all(): pl.pallas_call(functools.partial(reduce_kernel, sources), out_shape=jax.S...  40.1 us
    pallas_call x1, Pallas kernels, local(): pl.pallas_call(functools.partial(main_kernel, total_points, own_rows), ou...  37.7 us
    pallas_call x1, Pallas kernels, gather_all(): pl.pallas_call(functools.partial(gather_kernel, sources), out_shape=(jax....  28.1 us

profile of v7, /device:TPU:0, one launch (start us, length us, event | category | flops | bytes accessed | tf_op | source)
XLA Modules:
  0.0 108.7 jit_solution(15622427727257090049)
XLA Ops:
  0.6 28.1 %shard_map.113 = (bf16[2,1024,1024]{2,1,0:T(8,128)(2,1)}, s32[4,8,128]{2,1,0:T(8,128)}, f32[4,8,128]{2,1,0:T(8,128)}) custom-call(bf16[128,1024]{1,0:T(8,128)(2,1)} %re_ref.1, bf16[128,1024]{1,0:T(8,128)(2,1)} %im_ref.1, s32[1,8]{1,0:T(1,128)} %bitcast.11, s32[1,8]{1,0:T(1,128)} %bitcast.12, f32[1,8]{1,0:T(1,128)} %bitcast.13), custom_call_target="tpu_custom_call" | custom-call | tf_op jit(solution)/shard_map/pallas_call | solution.py:709
  28.8 37.7 %shard_map.114 = bf16[2,4,256,1024]{3,2,1,0:T(8,128)(2,1)} custom-call(s32[4,8,128]{2,1,0:T(8,128)} %get-tuple-element.5.cent_ref, f32[4,8,128]{2,1,0:T(8,128)} %get-tuple-element.6.weight_ref, bf16[2,1024,1024]{2,1,0:T(8,128)(2,1)} %get-tuple-element.7.spec_hbm, bf16[1024,1024]{1,0:T(8,128)(2,1)} %constant.8.clone.cos_ref, ...), custom_call_target="tpu_custom_call" | custom-call | tf_op jit(solution)/shard_map/pallas_call | solution.py:823
  66.5 40.1 %shard_map.115 = bf16[2,128,1024]{2,1,0:T(8,128)(2,1)} custom-call(bf16[2,4,2,2,2,32,1024]{6,5,4,3,2,1,0:T(8,128)(2,1)} %bitcast.10), custom_call_target="tpu_custom_call" | custom-call | tf_op jit(solution)/shard_map/pallas_call | solution.py:749
  106.5 2.1 %bitcast_convert_fusion = (f32[128,1024]{1,0:T(8,128)}, f32[128,1024]{1,0:T(8,128)}) fusion(bf16[2,128,1024]{2,1,0:T(8,128)(2,1)} %shard_map.115), kind=kLoop, calls=%fused_computation | loop fusion | flops 262144 | bytes 1572864 | tf_op jit(solution)/shard_map/convert_element_type | solution.py:782
